TPU v7x, 32 devices: a whole 2x2x4 slice. The times are simulated.
32 devices in a mesh: dp: 16 (over z, y, core), mp: 2 (over x).
Axes of the slice: x: 2, y: 2, z: 4, core: 2. Of those that a mesh axis runs over, the one named last changes fastest.
Arguments:
- tokens: bfloat16 [64, 512, 1024], P('dp'), may hold values from -6 to 6
- cotangent: bfloat16 [64, 512, 1024], P('dp', None, 'mp'), may hold values from -6 to 6
- segment_ids: int32 [64, 512], P('dp'), may hold values from 0 to 3, as said below
- positions: int32 [64, 512], P('dp'), may hold values from 0 to 1725, as said below
- attn_gain: bfloat16 [1024], replicated, may hold values from 0.099609375 to 1.8984375
- w_query: bfloat16 [1024, 1024], P('dp', 'mp'), may hold values from -0.1875 to 0.1875
- key_value_weight: bfloat16 [1024, 8, 128], P('dp', 'mp'), may hold values from -0.1875 to 0.1875
- w_out: bfloat16 [1024, 1024], P('mp', 'dp'), may hold values from -1.5 to 1.5
- qk_gain: bfloat16 [2, 64], replicated, may hold values from 0.099609375 to 1.8984375
- ffn_gain: bfloat16 [1024], replicated, may hold values from 0.099609375 to 1.8984375
- w_gateup: bfloat16 [1024, 2, 4608], P('dp', None, 'mp'), may hold values from -0.1875 to 0.1875
- w_down: bfloat16 [4608, 1024], P('mp', 'dp'), may hold values from -0.09375 to 0.09375
Outputs:
- mixed: bfloat16 [64, 512, 1024], P('dp', None, 'mp')
- tokens_grad: float32 [64, 512, 1024], P('dp', None, 'mp')
- attn_gain_grad: float32 [1024], replicated
- w_query_grad: float32 [1024, 1024], P('dp', 'mp')
- w_keyval_grad: float32 [1024, 8, 128], P('dp', 'mp')
- w_out_grad: float32 [1024, 1024], P('mp', 'dp')
- qk_gain_grad: float32 [2, 64], replicated
- ffn_gain_grad: float32 [1024], replicated
- w_gateup_grad: float32 [1024, 2, 4608], P('dp', None, 'mp')
- w_down_grad: float32 [4608, 1024], P('mp', 'dp')
Inputs may be any that keep to these rules, and one draw needn't show every extreme that they name: `segment_ids`: each sequence holds four documents numbered 0 to 3 in order, each of one token or more. `positions`: positions rise by one within a document and start at 0, except that a sequence's first document may continue one begun before it, from an offset of at most 1535; the largest position is 1725.
All inputs are finite; a program needn't handle non-finite values.
Results may differ from a plain program's by a relative error of at most 0.017.
Values may be sent and summed in bfloat16 or wider, within the bound.
A program may use at most 256 MiB of HBM per device.

v0:
```python
import jax
import jax.numpy as jnp
from jax import lax
from jax.sharding import PartitionSpec as P

MODEL_WIDTH = 1024
HEAD_SIZE = 64


epsilon = 1e-05
rope_base = 1000000.0


def rotate_table(place):
    half = HEAD_SIZE // 2
    frequency = rope_base ** (-(jnp.arange(half, dtype=jnp.float32) * 2.0 / HEAD_SIZE))
    angle = place.astype(jnp.float32)[:, None] * frequency[None, :]
    return (jnp.cos(angle)[:, None, :], jnp.sin(angle)[:, None, :])


def rotate(value, cosine, sine):
    half = HEAD_SIZE // 2
    first, second = (value[..., :half], value[..., half:])
    return jnp.concatenate(
        [first * cosine - second * sine, second * cosine + first * sine], axis=-1
    )


def unrotate(grad, cosine, sine):
    half = HEAD_SIZE // 2
    first, second = (grad[..., :half], grad[..., half:])
    return jnp.concatenate(
        [first * cosine + second * sine, second * cosine - first * sine], axis=-1
    )


def head_norm(value, gain):
    scale = lax.rsqrt(jnp.mean(value * value, axis=-1, keepdims=True) + epsilon)
    unit = value * scale
    return (unit * gain, unit, scale)


def head_norm_back(grad, unit, scale, gain):
    scaled = grad * gain
    inner = jnp.mean(unit * scaled, axis=-1, keepdims=True)
    return (scale * (scaled - unit * inner), jnp.sum(grad * unit, axis=(0, 1)))


def slice_norm_back(grad, unit, scale, gain):
    scaled = grad * gain
    inner = lax.psum(jnp.sum(unit * scaled, axis=-1, keepdims=True), "mp")
    return (scale * (scaled - unit * (inner / MODEL_WIDTH)), jnp.sum(grad * unit, axis=0))


def branch_sum(term):
    return lax.psum_scatter(term, "mp", scatter_dimension=1, tiled=True)


def normed_grad(term):
    return lax.psum_scatter(term, "mp", scatter_dimension=1, tiled=True)


def whole_grad(value):
    return lax.all_gather(value, "mp", axis=1, tiled=True)


def score_block(query_rot, key_rot, mask):
    length, kv_heads = (key_rot.shape[0], key_rot.shape[1])
    grouped = query_rot.reshape(length, kv_heads, -1, HEAD_SIZE)
    scores = jnp.einsum(
        "qhgd,khd->hgqk", grouped, key_rot, preferred_element_type=jnp.float32
    ) * HEAD_SIZE ** (-0.5)
    return (grouped, jnp.where(mask, scores, -1e30))


def attend(query_rot, key_rot, values, mask):
    length = query_rot.shape[0]
    grouped, scores = score_block(query_rot, key_rot, mask)
    top = jnp.max(scores, axis=-1, keepdims=True)
    expo = jnp.exp(scores - top)
    total = jnp.sum(expo, axis=-1, keepdims=True)
    weights = (expo / total).astype(jnp.bfloat16)
    attended = jnp.einsum("hgqk,khd->qhgd", weights, values, preferred_element_type=jnp.float32)
    return (attended.reshape(length, -1).astype(jnp.bfloat16), top + jnp.log(total))


def attend_back(query_rot, key_rot, values, mask, logsum, grad_out):
    length, kv_heads = (key_rot.shape[0], key_rot.shape[1])
    grouped, scores = score_block(query_rot, key_rot, mask)
    grad_grouped = grad_out.reshape(length, kv_heads, -1, HEAD_SIZE)
    probs = jnp.exp(scores - logsum)
    weights = probs.astype(jnp.bfloat16)
    grad_probs = jnp.einsum(
        "qhgd,khd->hgqk", grad_grouped, values, preferred_element_type=jnp.float32
    )
    inner = jnp.sum(probs * grad_probs, axis=-1, keepdims=True)
    grad_scores = (probs * (grad_probs - inner)).astype(jnp.bfloat16)
    grad_values = jnp.einsum(
        "hgqk,qhgd->khd", weights, grad_grouped, preferred_element_type=jnp.float32
    )
    grad_query = jnp.einsum(
        "hgqk,khd->qhgd", grad_scores, key_rot, preferred_element_type=jnp.float32
    ) * HEAD_SIZE ** (-0.5)
    grad_key = jnp.einsum(
        "hgqk,qhgd->khd", grad_scores, grouped, preferred_element_type=jnp.float32
    ) * HEAD_SIZE ** (-0.5)
    return (grad_query.reshape(length, -1, HEAD_SIZE), grad_key, grad_values)


def body(
    tokens,
    cotangent,
    segment_ids,
    positions,
    attn_gain,
    w_query,
    key_value_weight,
    w_out,
    qk_gain,
    ffn_gain,
    w_gateup,
    w_down,
):
    parts = lax.axis_size("mp")
    width = MODEL_WIDTH // parts
    offset = lax.axis_index("mp") * width
    kv_heads = key_value_weight.shape[1]
    ff_local = w_gateup.shape[2]
    head_cols = w_query.shape[1]
    gain_first = attn_gain.astype(jnp.float32)
    gain_second = ffn_gain.astype(jnp.float32)
    first_part = lax.dynamic_slice_in_dim(gain_first, offset, width)
    second_part = lax.dynamic_slice_in_dim(gain_second, offset, width)
    query_gain = qk_gain[0].astype(jnp.float32)
    key_gain = qk_gain[1].astype(jnp.float32)

    def micro(carry, item):
        block, grad_slice, segment, place = item
        forward_set = (
            lax.all_gather(w_query, "dp", axis=0, tiled=True),
            lax.all_gather(key_value_weight, "dp", axis=0, tiled=True),
            lax.all_gather(w_out, "dp", axis=1, tiled=True),
            lax.all_gather(w_gateup, "dp", axis=0, tiled=True),
            lax.all_gather(w_down, "dp", axis=1, tiled=True),
        )
        query_w, key_value_matrix, out_w, gateup_w, down_w = forward_set
        length = block.shape[0]
        order = jnp.arange(length)
        mask = (segment[:, None] == segment[None, :]) & (order[None, :] <= order[:, None])
        cosine, sine = rotate_table(place)
        block_f = block.astype(jnp.float32)
        scale_first = lax.rsqrt(jnp.mean(block_f * block_f, axis=-1, keepdims=True) + epsilon)
        first_normed_input = (block_f * scale_first * gain_first).astype(jnp.bfloat16)
        query_raw = jnp.dot(
            first_normed_input, query_w, preferred_element_type=jnp.float32
        ).reshape(length, -1, HEAD_SIZE)
        keyval_raw = jnp.dot(
            first_normed_input,
            key_value_matrix.reshape(MODEL_WIDTH, -1),
            preferred_element_type=jnp.float32,
        ).reshape(length, kv_heads, 2 * HEAD_SIZE)
        query_normed, query_unit, query_scale = head_norm(query_raw, query_gain)
        key_normed, key_unit, key_scale = head_norm(keyval_raw[..., :HEAD_SIZE], key_gain)
        query_rot = rotate(query_normed, cosine, sine).astype(jnp.bfloat16)
        key_rot = rotate(key_normed, cosine, sine).astype(jnp.bfloat16)
        values = keyval_raw[..., HEAD_SIZE:].astype(jnp.bfloat16)
        attended, logsum = attend(query_rot, key_rot, values, mask)
        own = lax.dynamic_slice_in_dim(block_f, offset, width, 1)
        resid = own + branch_sum(jnp.dot(attended, out_w, preferred_element_type=jnp.float32))
        resid_all = lax.all_gather(resid, "mp", axis=1, tiled=True)
        scale_second = lax.rsqrt(jnp.mean(resid_all * resid_all, axis=-1, keepdims=True) + epsilon)
        normed_second = (resid_all * scale_second * gain_second).astype(jnp.bfloat16)
        unit_second = resid * scale_second
        gateup = jnp.dot(
            normed_second,
            gateup_w.reshape(MODEL_WIDTH, 2 * ff_local),
            preferred_element_type=jnp.float32,
        )
        gate = gateup[:, :ff_local]
        upper = gateup[:, ff_local:]
        sigmoid_gate = jax.nn.sigmoid(gate)
        hidden = (gate * sigmoid_gate * upper).astype(jnp.bfloat16)
        mixed = (
            resid + branch_sum(jnp.dot(hidden, down_w, preferred_element_type=jnp.float32))
        ).astype(jnp.bfloat16)
        back_set = (
            lax.all_gather(w_query, "dp", axis=0, tiled=True),
            lax.all_gather(key_value_weight, "dp", axis=0, tiled=True),
            lax.all_gather(w_out, "dp", axis=1, tiled=True),
            lax.all_gather(w_gateup, "dp", axis=0, tiled=True),
            lax.all_gather(w_down, "dp", axis=1, tiled=True),
        )
        query_back, keyval_back, out_back, gateup_back, down_back = back_set
        grad_whole = whole_grad(grad_slice)
        down_grad = jnp.einsum("tf,td->fd", hidden, grad_whole, preferred_element_type=jnp.float32)
        grad_hidden = jnp.einsum(
            "td,fd->tf", grad_whole, down_back, preferred_element_type=jnp.float32
        )
        grad_gate = grad_hidden * upper * sigmoid_gate * (1.0 + gate * (1.0 - sigmoid_gate))
        grad_upper = grad_hidden * gate * sigmoid_gate
        grad_gateup = jnp.concatenate([grad_gate, grad_upper], axis=-1).astype(jnp.bfloat16)
        gateup_grad = jnp.einsum(
            "td,tf->df", normed_second, grad_gateup, preferred_element_type=jnp.float32
        )
        grad_second = normed_grad(
            jnp.einsum(
                "tf,df->td",
                grad_gateup,
                gateup_back.reshape(MODEL_WIDTH, 2 * ff_local),
                preferred_element_type=jnp.float32,
            )
        )
        back_second, second_gain = slice_norm_back(
            grad_second, unit_second, scale_second, second_part
        )
        grad_resid = back_second + grad_slice.astype(jnp.float32)
        grad_branch = whole_grad(grad_resid.astype(jnp.bfloat16))
        out_grad = jnp.einsum(
            "tk,td->kd", attended, grad_branch, preferred_element_type=jnp.float32
        )
        grad_attended = (
            jnp.einsum("td,kd->tk", grad_branch, out_back, preferred_element_type=jnp.float32)
            .astype(jnp.bfloat16)
            .reshape(length, -1, HEAD_SIZE)
        )
        grad_query, grad_key, grad_values = attend_back(
            query_rot, key_rot, values, mask, logsum, grad_attended
        )
        query_raw_grad, query_gain_grad = head_norm_back(
            unrotate(grad_query, cosine, sine), query_unit, query_scale, query_gain
        )
        key_raw_grad, key_gain_grad = head_norm_back(
            unrotate(grad_key, cosine, sine), key_unit, key_scale, key_gain
        )
        grad_query_raw = query_raw_grad.reshape(length, -1).astype(jnp.bfloat16)
        grad_keyval_raw = (
            jnp.concatenate([key_raw_grad, grad_values], axis=-1)
            .reshape(length, -1)
            .astype(jnp.bfloat16)
        )
        query_grad = jnp.einsum(
            "td,tk->dk", first_normed_input, grad_query_raw, preferred_element_type=jnp.float32
        )
        keyval_grad = jnp.einsum(
            "td,tk->dk", first_normed_input, grad_keyval_raw, preferred_element_type=jnp.float32
        )
        first_term = jnp.einsum(
            "tk,dk->td", grad_query_raw, query_back, preferred_element_type=jnp.float32
        )
        first_term = first_term + jnp.einsum(
            "tk,dk->td",
            grad_keyval_raw,
            keyval_back.reshape(MODEL_WIDTH, -1),
            preferred_element_type=jnp.float32,
        )
        grad_first = normed_grad(first_term)
        back_first, first_gain = slice_norm_back(
            grad_first, own * scale_first, scale_first, first_part
        )
        grad_input = back_first + grad_resid
        terms = (
            query_grad,
            keyval_grad,
            out_grad,
            gateup_grad,
            down_grad,
            first_gain,
            second_gain,
            jnp.stack([query_gain_grad, key_gain_grad]),
        )
        return (jax.tree.map(jnp.add, carry, terms), (mixed, grad_input))

    start = (
        jnp.zeros((MODEL_WIDTH, head_cols), jnp.float32),
        jnp.zeros((MODEL_WIDTH, kv_heads * 2 * HEAD_SIZE), jnp.float32),
        jnp.zeros((head_cols, MODEL_WIDTH), jnp.float32),
        jnp.zeros((MODEL_WIDTH, 2 * ff_local), jnp.float32),
        jnp.zeros((ff_local, MODEL_WIDTH), jnp.float32),
        jnp.zeros((width,), jnp.float32),
        jnp.zeros((width,), jnp.float32),
        jnp.zeros((2, HEAD_SIZE), jnp.float32),
    )
    totals, (mixed, grad_input) = lax.scan(
        micro, start, (tokens, cotangent, segment_ids, positions)
    )
    query_sum, keyval_sum, out_sum, gateup_sum, down_sum = (
        lax.psum_scatter(
            totals[0].astype(jnp.bfloat16), "dp", scatter_dimension=0, tiled=True
        ).astype(jnp.float32),
        lax.psum_scatter(
            totals[1].reshape(MODEL_WIDTH, kv_heads, 2 * HEAD_SIZE).astype(jnp.bfloat16),
            "dp",
            scatter_dimension=0,
            tiled=True,
        ).astype(jnp.float32),
        lax.psum_scatter(
            totals[2].astype(jnp.bfloat16), "dp", scatter_dimension=1, tiled=True
        ).astype(jnp.float32),
        lax.psum_scatter(
            totals[3].reshape(MODEL_WIDTH, 2, ff_local).astype(jnp.bfloat16),
            "dp",
            scatter_dimension=0,
            tiled=True,
        ).astype(jnp.float32),
        lax.psum_scatter(
            totals[4].astype(jnp.bfloat16), "dp", scatter_dimension=1, tiled=True
        ).astype(jnp.float32),
    )
    first_full = lax.dynamic_update_slice_in_dim(
        jnp.zeros((MODEL_WIDTH,), jnp.float32), totals[5], offset, 0
    )
    second_full = lax.dynamic_update_slice_in_dim(
        jnp.zeros((MODEL_WIDTH,), jnp.float32), totals[6], offset, 0
    )
    first_sum, second_sum, pair_sum = lax.psum((first_full, second_full, totals[7]), ("dp", "mp"))
    return (
        mixed,
        grad_input,
        first_sum,
        query_sum,
        keyval_sum,
        out_sum,
        pair_sum,
        second_sum,
        gateup_sum,
        down_sum,
    )


def solution(mesh):
    placed = (
        P("dp", None, None),
        P("dp", None, "mp"),
        P("dp", None),
        P("dp", None),
        P(),
        P("dp", "mp"),
        P("dp", "mp", None),
        P("mp", "dp"),
        P(),
        P(),
        P("dp", None, "mp"),
        P("mp", "dp"),
    )
    return jax.shard_map(
        body,
        mesh=mesh,
        in_specs=placed,
        out_specs=(
            P("dp", None, "mp"),
            P("dp", None, "mp"),
            P(),
            P("dp", "mp"),
            P("dp", "mp", None),
            P("mp", "dp"),
            P(),
            P(),
            P("dp", None, "mp"),
            P("mp", "dp"),
        ),
        check_vma=False,
    )
```

profile of v0, /device:TPU:0, one launch (start us, length us, event | category | flops | bytes accessed | tf_op | source)
XLA Modules:
  0.0 2487.4 jit_solution(3685616672598107089)
XLA Ops:
  15.0 2057.6 %while.31 = (s32[]{:T(128)}, f32[1024,512]{1,0:T(8,128)}, f32[1024,512]{1,0:T(8,128)}, f32[512,1024]{1,0:T(8,128)}, f32[1024,4608]{1,0:T(8,128)}, /*index=5*/f32...) while((s32[]{:T(128)}, f32[1024,512]{1,0:T(8,128)}, ...), condition=%wide.region_22.23_spmd.clone, body=%wide.region_0.22_spmd.clone.sunk | while | flops 28317990912 | bytes 563335424 | solution.py:283
  20.0 38.6 %all-gather.13.cloned.1.call-done = bf16[1024,512]{1,0:T(8,128)(2,1)} async-done(((bf16[64,512]{1,0:T(8,128)(2,1)}), bf16[1024,512]{1,0:T(8,128)(2,1)}) %all-gather.13.cloned.1.call-update) | async-done | bytes 1048592 | tf_op jit(solution)/shard_map/while/body/eval_jaxpr/all_gather | solution.py:140
  62.2 36.1 %all-gather.15.cloned.1.call-done = bf16[1024,4,128]{2,0,1:T(8,128)(2,1)} async-done(((bf16[64,4,128]{2,0,1:T(8,128)(2,1)}), bf16[1024,4,128]{2,0,1:T(8,128)(2,1)}) %all-gather.15.cloned.1.call-update) | async-done | bytes 1048592 | tf_op jit(solution)/shard_map/while/body/eval_jaxpr/all_gather | solution.py:141
  110.3 27.1 %all-gather.19.cloned.1.call-done = bf16[512,1024]{0,1:T(8,128)(2,1)} async-done(((bf16[512,64]{0,1:T(8,128)(2,1)}), bf16[512,1024]{0,1:T(8,128)(2,1)}) %all-gather.19.cloned.1.call-update) | async-done | bytes 1048592 | tf_op jit(solution)/shard_map/while/body/eval_jaxpr/all_gather | solution.py:142
  142.2 29.4 %reduce-scatter.14.cloned.1.call-done = f32[512,512]{1,0:T(8,128)} async-done(((f32[512,1024]{1,0:T(8,128)}), f32[512,512]{1,0:T(8,128)}) %reduce-scatter.14.cloned.1.call-update) | async-done | bytes 1048592 | tf_op jit(solution)/shard_map/while/body/eval_jaxpr/reduce_scatter | solution.py:56
  177.5 29.8 %all-gather.21.cloned.1.call-done = f32[512,1024]{1,0:T(8,128)} async-done(((f32[512,512]{1,0:T(8,128)}), f32[512,1024]{1,0:T(8,128)}) %all-gather.21.cloned.1.call-update) | async-done | bytes 2097168 | tf_op jit(solution)/shard_map/while/body/eval_jaxpr/all_gather | solution.py:170
  209.1 82.1 %all-gather.17.cloned.1.call-done = bf16[1024,2,2304]{2,1,0:T(2,128)(2,1)} async-done(((bf16[64,2,2304]{2,1,0:T(2,128)(2,1)}), bf16[1024,2,2304]{2,1,0:T(2,128)(2,1)}) %all-gather.17.cloned.1.call-update) | async-done | bytes 9437200 | tf_op jit(solution)/shard_map/while/body/eval_jaxpr/all_gather | solution.py:143
  291.2 9.0 copy.66
  300.2 11.6 fusion.155
  312.8 56.0 %all-gather.23.cloned.1.call-done = bf16[2304,1024]{0,1:T(8,128)(2,1)} async-done(((bf16[2304,64]{0,1:T(8,128)(2,1)}), bf16[2304,1024]{0,1:T(8,128)(2,1)}) %all-gather.23.cloned.1.call-update) | async-done | bytes 4718608 | tf_op jit(solution)/shard_map/while/body/eval_jaxpr/all_gather | solution.py:191
  368.8 9.4 multiply_convert_fusion.20
  380.4 8.7 fusion.156
  389.1 30.5 %reduce-scatter.16.cloned.1.call-done = f32[512,512]{1,0:T(8,128)} async-done(((f32[512,1024]{1,0:T(8,128)}), f32[512,512]{1,0:T(8,128)}) %reduce-scatter.16.cloned.1.call-update) | async-done | bytes 1048592 | tf_op jit(solution)/shard_map/while/body/eval_jaxpr/reduce_scatter | solution.py:60
  437.6 13.6 all-gather.27.cloned.1.call-done
  482.3 15.6 select_add_fusion.17
  510.6 8.8 reduce-scatter.18.cloned.1.call-done
  534.1 36.2 %all-gather.13.cloned.1.call-done = bf16[1024,512]{1,0:T(8,128)(2,1)} async-done(((bf16[64,512]{1,0:T(8,128)(2,1)}), bf16[1024,512]{1,0:T(8,128)(2,1)}) %all-gather.13.cloned.1.call-update) | async-done | bytes 1048592 | tf_op jit(solution)/shard_map/while/body/eval_jaxpr/all_gather | solution.py:140
  574.0 35.9 %all-gather.15.cloned.1.call-done = bf16[1024,4,128]{2,0,1:T(8,128)(2,1)} async-done(((bf16[64,4,128]{2,0,1:T(8,128)(2,1)}), bf16[1024,4,128]{2,0,1:T(8,128)(2,1)}) %all-gather.15.cloned.1.call-update) | async-done | bytes 1048592 | tf_op jit(solution)/shard_map/while/body/eval_jaxpr/all_gather | solution.py:141
  621.9 26.9 %all-gather.19.cloned.1.call-done = bf16[512,1024]{0,1:T(8,128)(2,1)} async-done(((bf16[512,64]{0,1:T(8,128)(2,1)}), bf16[512,1024]{0,1:T(8,128)(2,1)}) %all-gather.19.cloned.1.call-update) | async-done | bytes 1048592 | tf_op jit(solution)/shard_map/while/body/eval_jaxpr/all_gather | solution.py:142
  653.6 29.3 %reduce-scatter.14.cloned.1.call-done = f32[512,512]{1,0:T(8,128)} async-done(((f32[512,1024]{1,0:T(8,128)}), f32[512,512]{1,0:T(8,128)}) %reduce-scatter.14.cloned.1.call-update) | async-done | bytes 1048592 | tf_op jit(solution)/shard_map/while/body/eval_jaxpr/reduce_scatter | solution.py:56
  688.8 29.9 %all-gather.21.cloned.1.call-done = f32[512,1024]{1,0:T(8,128)} async-done(((f32[512,512]{1,0:T(8,128)}), f32[512,1024]{1,0:T(8,128)}) %all-gather.21.cloned.1.call-update) | async-done | bytes 2097168 | tf_op jit(solution)/shard_map/while/body/eval_jaxpr/all_gather | solution.py:170
  720.5 82.1 %all-gather.17.cloned.1.call-done = bf16[1024,2,2304]{2,1,0:T(2,128)(2,1)} async-done(((bf16[64,2,2304]{2,1,0:T(2,128)(2,1)}), bf16[1024,2,2304]{2,1,0:T(2,128)(2,1)}) %all-gather.17.cloned.1.call-update) | async-done | bytes 9437200 | tf_op jit(solution)/shard_map/while/body/eval_jaxpr/all_gather | solution.py:143
  802.6 9.0 copy.66
  811.6 11.6 fusion.155
  824.2 55.8 %all-gather.23.cloned.1.call-done = bf16[2304,1024]{0,1:T(8,128)(2,1)} async-done(((bf16[2304,64]{0,1:T(8,128)(2,1)}), bf16[2304,1024]{0,1:T(8,128)(2,1)}) %all-gather.23.cloned.1.call-update) | async-done | bytes 4718608 | tf_op jit(solution)/shard_map/while/body/eval_jaxpr/all_gather | solution.py:191
  880.1 9.4 multiply_convert_fusion.20
  900.4 30.5 %reduce-scatter.16.cloned.1.call-done = f32[512,512]{1,0:T(8,128)} async-done(((f32[512,1024]{1,0:T(8,128)}), f32[512,512]{1,0:T(8,128)}) %reduce-scatter.16.cloned.1.call-update) | async-done | bytes 1048592 | tf_op jit(solution)/shard_map/while/body/eval_jaxpr/reduce_scatter | solution.py:60
  948.9 13.6 all-gather.27.cloned.1.call-done
  985.6 11.0 select_add_fusion.18
  996.6 20.5 select_add_fusion.17
  1047.5 36.0 %all-gather.13.cloned.1.call-done = bf16[1024,512]{1,0:T(8,128)(2,1)} async-done(((bf16[64,512]{1,0:T(8,128)(2,1)}), bf16[1024,512]{1,0:T(8,128)(2,1)}) %all-gather.13.cloned.1.call-update) | async-done | bytes 1048592 | tf_op jit(solution)/shard_map/while/body/eval_jaxpr/all_gather | solution.py:140
  1087.1 35.9 %all-gather.15.cloned.1.call-done = bf16[1024,4,128]{2,0,1:T(8,128)(2,1)} async-done(((bf16[64,4,128]{2,0,1:T(8,128)(2,1)}), bf16[1024,4,128]{2,0,1:T(8,128)(2,1)}) %all-gather.15.cloned.1.call-update) | async-done | bytes 1048592 | tf_op jit(solution)/shard_map/while/body/eval_jaxpr/all_gather | solution.py:141
  1135.0 26.9 %all-gather.19.cloned.1.call-done = bf16[512,1024]{0,1:T(8,128)(2,1)} async-done(((bf16[512,64]{0,1:T(8,128)(2,1)}), bf16[512,1024]{0,1:T(8,128)(2,1)}) %all-gather.19.cloned.1.call-update) | async-done | bytes 1048592 | tf_op jit(solution)/shard_map/while/body/eval_jaxpr/all_gather | solution.py:142
  1166.8 29.3 %reduce-scatter.14.cloned.1.call-done = f32[512,512]{1,0:T(8,128)} async-done(((f32[512,1024]{1,0:T(8,128)}), f32[512,512]{1,0:T(8,128)}) %reduce-scatter.14.cloned.1.call-update) | async-done | bytes 1048592 | tf_op jit(solution)/shard_map/while/body/eval_jaxpr/reduce_scatter | solution.py:56
  1202.3 29.6 %all-gather.21.cloned.1.call-done = f32[512,1024]{1,0:T(8,128)} async-done(((f32[512,512]{1,0:T(8,128)}), f32[512,1024]{1,0:T(8,128)}) %all-gather.21.cloned.1.call-update) | async-done | bytes 2097168 | tf_op jit(solution)/shard_map/while/body/eval_jaxpr/all_gather | solution.py:170
  1233.7 82.1 %all-gather.17.cloned.1.call-done = bf16[1024,2,2304]{2,1,0:T(2,128)(2,1)} async-done(((bf16[64,2,2304]{2,1,0:T(2,128)(2,1)}), bf16[1024,2,2304]{2,1,0:T(2,128)(2,1)}) %all-gather.17.cloned.1.call-update) | async-done | bytes 9437200 | tf_op jit(solution)/shard_map/while/body/eval_jaxpr/all_gather | solution.py:143
  1315.7 9.0 copy.66
  1324.7 11.7 fusion.155
  1337.4 56.0 %all-gather.23.cloned.1.call-done = bf16[2304,1024]{0,1:T(8,128)(2,1)} async-done(((bf16[2304,64]{0,1:T(8,128)(2,1)}), bf16[2304,1024]{0,1:T(8,128)(2,1)}) %all-gather.23.cloned.1.call-update) | async-done | bytes 4718608 | tf_op jit(solution)/shard_map/while/body/eval_jaxpr/all_gather | solution.py:191
  1393.4 9.4 multiply_convert_fusion.20
  1413.8 30.5 %reduce-scatter.16.cloned.1.call-done = f32[512,512]{1,0:T(8,128)} async-done(((f32[512,1024]{1,0:T(8,128)}), f32[512,512]{1,0:T(8,128)}) %reduce-scatter.16.cloned.1.call-update) | async-done | bytes 1048592 | tf_op jit(solution)/shard_map/while/body/eval_jaxpr/reduce_scatter | solution.py:60
  1462.3 13.6 all-gather.27.cloned.1.call-done
  1498.7 11.0 select_add_fusion.18
  1509.7 20.4 select_add_fusion.17
  1560.7 35.8 %all-gather.13.cloned.1.call-done = bf16[1024,512]{1,0:T(8,128)(2,1)} async-done(((bf16[64,512]{1,0:T(8,128)(2,1)}), bf16[1024,512]{1,0:T(8,128)(2,1)}) %all-gather.13.cloned.1.call-update) | async-done | bytes 1048592 | tf_op jit(solution)/shard_map/while/body/eval_jaxpr/all_gather | solution.py:140
  1600.2 36.1 %all-gather.15.cloned.1.call-done = bf16[1024,4,128]{2,0,1:T(8,128)(2,1)} async-done(((bf16[64,4,128]{2,0,1:T(8,128)(2,1)}), bf16[1024,4,128]{2,0,1:T(8,128)(2,1)}) %all-gather.15.cloned.1.call-update) | async-done | bytes 1048592 | tf_op jit(solution)/shard_map/while/body/eval_jaxpr/all_gather | solution.py:141
  1648.2 26.9 %all-gather.19.cloned.1.call-done = bf16[512,1024]{0,1:T(8,128)(2,1)} async-done(((bf16[512,64]{0,1:T(8,128)(2,1)}), bf16[512,1024]{0,1:T(8,128)(2,1)}) %all-gather.19.cloned.1.call-update) | async-done | bytes 1048592 | tf_op jit(solution)/shard_map/while/body/eval_jaxpr/all_gather | solution.py:142
  1680.0 29.3 %reduce-scatter.14.cloned.1.call-done = f32[512,512]{1,0:T(8,128)} async-done(((f32[512,1024]{1,0:T(8,128)}), f32[512,512]{1,0:T(8,128)}) %reduce-scatter.14.cloned.1.call-update) | async-done | bytes 1048592 | tf_op jit(solution)/shard_map/while/body/eval_jaxpr/reduce_scatter | solution.py:56
  1715.4 29.6 %all-gather.21.cloned.1.call-done = f32[512,1024]{1,0:T(8,128)} async-done(((f32[512,512]{1,0:T(8,128)}), f32[512,1024]{1,0:T(8,128)}) %all-gather.21.cloned.1.call-update) | async-done | bytes 2097168 | tf_op jit(solution)/shard_map/while/body/eval_jaxpr/all_gather | solution.py:170
  1746.9 82.2 %all-gather.17.cloned.1.call-done = bf16[1024,2,2304]{2,1,0:T(2,128)(2,1)} async-done(((bf16[64,2,2304]{2,1,0:T(2,128)(2,1)}), bf16[1024,2,2304]{2,1,0:T(2,128)(2,1)}) %all-gather.17.cloned.1.call-update) | async-done | bytes 9437200 | tf_op jit(solution)/shard_map/while/body/eval_jaxpr/all_gather | solution.py:143
  1829.1 9.0 copy.66
  1838.1 11.7 fusion.155
  1850.6 56.0 %all-gather.23.cloned.1.call-done = bf16[2304,1024]{0,1:T(8,128)(2,1)} async-done(((bf16[2304,64]{0,1:T(8,128)(2,1)}), bf16[2304,1024]{0,1:T(8,128)(2,1)}) %all-gather.23.cloned.1.call-update) | async-done | bytes 4718608 | tf_op jit(solution)/shard_map/while/body/eval_jaxpr/all_gather | solution.py:191
  1906.6 9.4 multiply_convert_fusion.20
  1926.9 30.5 %reduce-scatter.16.cloned.1.call-done = f32[512,512]{1,0:T(8,128)} async-done(((f32[512,1024]{1,0:T(8,128)}), f32[512,512]{1,0:T(8,128)}) %reduce-scatter.16.cloned.1.call-update) | async-done | bytes 1048592 | tf_op jit(solution)/shard_map/while/body/eval_jaxpr/reduce_scatter | solution.py:60
  1975.5 13.6 all-gather.27.cloned.1.call-done
  2012.0 11.0 select_add_fusion.18
  2023.0 20.8 select_add_fusion.17
  2080.9 11.3 convert_element_type.225
  2092.3 13.2 convert_element_type.226
  2115.5 39.1 %all-reduce.2 = (f32[1024]{0:T(1024)}, f32[2,64]{1,0:T(2,128)}, f32[1024]{0:T(1024)}) all-reduce(f32[1024]{0:T(1024)S(1)} %dynamic_update_slice.20, f32[2,64]{1,0:T(2,128)S(1)} %copy-done.47, f32[1024]{0:T(1024)S(1)} %dynamic_update_slice.21), channel_id=1, replica_groups=mesh['dp'=16,'mp'=2] {'dp','mp'}, use_global_device_ids=true, to_apply=%region_23.24 | all-reduce | flops 2176 | bytes 17408 | tf_op jit(solution)/shard_map/psum | solution.py:315
  2156.2 38.5 %reduce-scatter.10.cloned.1.call-done = bf16[512,64]{0,1:T(8,128)(2,1)} async-done(((bf16[512,1024]{0,1:T(8,128)(2,1)}), bf16[512,64]{0,1:T(8,128)(2,1)}) %reduce-scatter.10.cloned.1.call-update) | async-done | bytes 65552 | tf_op jit(solution)/shard_map/reduce_scatter | solution.py:296
  2196.2 202.2 %all-reduce.6.cloned.1.call-done = (bf16[1024,4,128]{2,1,0:T(4,128)(2,1)}, bf16[1024,2,2304]{2,1,0:T(2,128)(2,1)}) async-done(((bf16[1024,4,128]{2,1,0:T(4,128)(2,1)}, bf16[1024,2,2304]{2,1,0:T(2,128)(2,1)}), (bf16[1024,4,128]{2,1,0:T(4,128)(2,1)}, bf16[1024,2,2304]{2,1,0:T(2,128)(2,1)})) %all-reduce.6.cloned.1.call-update) | async-done | bytes 10485776
  2402.3 75.7 %reduce-scatter.12.cloned.1.call-done = bf16[2304,64]{0,1:T(8,128)(2,1)} async-done(((bf16[2304,1024]{0,1:T(8,128)(2,1)}), bf16[2304,64]{0,1:T(8,128)(2,1)}) %reduce-scatter.12.cloned.1.call-update) | async-done | bytes 294928 | tf_op jit(solution)/shard_map/reduce_scatter | solution.py:305
  (779 shorter events, 472.4 us)
Async XLA Ops:
  15.0 84.8 %copy-start.33 = (f32[1024]{0:T(1024)}, f32[1024]{0:T(1024)S(1)}, u32[]{:S(2)}) copy-start(f32[1024]{0:T(1024)S(1)} %get-tuple-element.908) | copy-start | bytes 12292 | tf_op jit(solution)/shard_map/while
  15.0 411.7 %copy-start.31 = (f32[512]{0:T(512)}, f32[512]{0:T(512)S(1)}, u32[]{:S(2)}) copy-start(f32[512]{0:T(512)S(1)} %get-tuple-element.921) | copy-start | bytes 6148 | tf_op jit(solution)/shard_map/while
  15.0 43.7 %all-gather.13.cloned.1.call-start = ((), (), s32[]{:S(2)}) async-start(), calls=%async_computation.11 | async-start | bytes 1114112 | tf_op jit(solution)/shard_map/while/body/eval_jaxpr/all_gather | solution.py:140
  15.7 82.6 %all-gather.15.cloned.1.call-start = ((), (), s32[]{:S(2)}) async-start(), calls=%async_computation.12 | async-start | bytes 1114112 | tf_op jit(solution)/shard_map/while/body/eval_jaxpr/all_gather | solution.py:141
  16.5 120.9 %all-gather.19.cloned.1.call-start = ((), (), s32[]{:S(2)}) async-start(), calls=%async_computation.14 | async-start | bytes 1114112 | tf_op jit(solution)/shard_map/while/body/eval_jaxpr/all_gather | solution.py:142
  17.2 154.4 %reduce-scatter.14.cloned.1.call-start = ((), (), s32[]{:S(2)}) async-start(), calls=%async_computation.15 | async-start | bytes 3145728 | tf_op jit(solution)/shard_map/while/body/eval_jaxpr/reduce_scatter | solution.py:56
  140.7 66.6 %all-gather.21.cloned.1.call-start = ((), (), s32[]{:S(2)}) async-start(), calls=%async_computation.16 | async-start | bytes 3145728 | tf_op jit(solution)/shard_map/while/body/eval_jaxpr/all_gather | solution.py:170
  174.0 117.2 %all-gather.17.cloned.1.call-start = ((), (), s32[]{:S(2)}) async-start(), calls=%async_computation.13 | async-start | bytes 10027008 | tf_op jit(solution)/shard_map/while/body/eval_jaxpr/all_gather | solution.py:143
  174.6 138.2 %all-gather.25.cloned.1.call-start = ((), (), s32[]{:S(2)}) async-start(), calls=%async_computation.18 | async-start | bytes 1572864 | tf_op jit(solution)/shard_map/while/body/eval_jaxpr/all_gather | solution.py:64
  176.5 192.3 %all-gather.23.cloned.1.call-start = ((), (), s32[]{:S(2)}) async-start(), calls=%async_computation.17 | async-start | bytes 5013504 | tf_op jit(solution)/shard_map/while/body/eval_jaxpr/all_gather | solution.py:191
  177.3 242.3 %reduce-scatter.16.cloned.1.call-start = ((), (), s32[]{:S(2)}) async-start(), calls=%async_computation.19 | async-start | bytes 3145728 | tf_op jit(solution)/shard_map/while/body/eval_jaxpr/reduce_scatter | solution.py:60
  209.1 217.6 %copy-start.25 = (f32[512]{0:T(512)}, f32[512]{0:T(512)S(1)}, u32[]{:S(2)}) copy-start(f32[512]{0:T(512)S(1)} %add_rsqrt_fusion.11) | copy-start | bytes 6148 | tf_op jit(solution)/shard_map/while
  389.1 62.2 %all-gather.27.cloned.1.call-start = ((), (), s32[]{:S(2)}) async-start(), calls=%async_computation.20 | async-start | bytes 1572864 | tf_op jit(solution)/shard_map/while/body/eval_jaxpr/all_gather | solution.py:64
  429.8 68.2 %reduce-scatter.20.cloned.1.call-start = ((), (), s32[]{:S(2)}) async-start(), calls=%async_computation.22 | async-start | bytes 3145728 | tf_op jit(solution)/shard_map/while/body/eval_jaxpr/reduce_scatter | solution.py:56
  437.6 81.8 %reduce-scatter.18.cloned.1.call-start = ((), (), s32[]{:S(2)}) async-start(), calls=%async_computation.21 | async-start | bytes 3145728 | tf_op jit(solution)/shard_map/while/body/eval_jaxpr/reduce_scatter | solution.py:60
  529.4 82.0 %copy-start.33 = (f32[1024]{0:T(1024)}, f32[1024]{0:T(1024)S(1)}, u32[]{:S(2)}) copy-start(f32[1024]{0:T(1024)S(1)} %get-tuple-element.908) | copy-start | bytes 12292 | tf_op jit(solution)/shard_map/while
  529.4 408.6 %copy-start.31 = (f32[512]{0:T(512)}, f32[512]{0:T(512)S(1)}, u32[]{:S(2)}) copy-start(f32[512]{0:T(512)S(1)} %get-tuple-element.921) | copy-start | bytes 6148 | tf_op jit(solution)/shard_map/while
  529.4 41.0 %all-gather.13.cloned.1.call-start = ((), (), s32[]{:S(2)}) async-start(), calls=%async_computation.11 | async-start | bytes 1114112 | tf_op jit(solution)/shard_map/while/body/eval_jaxpr/all_gather | solution.py:140
  530.1 79.8 %all-gather.15.cloned.1.call-start = ((), (), s32[]{:S(2)}) async-start(), calls=%async_computation.12 | async-start | bytes 1114112 | tf_op jit(solution)/shard_map/while/body/eval_jaxpr/all_gather | solution.py:141
  530.7 118.1 %all-gather.19.cloned.1.call-start = ((), (), s32[]{:S(2)}) async-start(), calls=%async_computation.14 | async-start | bytes 1114112 | tf_op jit(solution)/shard_map/while/body/eval_jaxpr/all_gather | solution.py:142
  531.3 151.7 %reduce-scatter.14.cloned.1.call-start = ((), (), s32[]{:S(2)}) async-start(), calls=%async_computation.15 | async-start | bytes 3145728 | tf_op jit(solution)/shard_map/while/body/eval_jaxpr/reduce_scatter | solution.py:56
  652.1 66.6 %all-gather.21.cloned.1.call-start = ((), (), s32[]{:S(2)}) async-start(), calls=%async_computation.16 | async-start | bytes 3145728 | tf_op jit(solution)/shard_map/while/body/eval_jaxpr/all_gather | solution.py:170
  685.4 117.2 %all-gather.17.cloned.1.call-start = ((), (), s32[]{:S(2)}) async-start(), calls=%async_computation.13 | async-start | bytes 10027008 | tf_op jit(solution)/shard_map/while/body/eval_jaxpr/all_gather | solution.py:143
  686.0 138.2 %all-gather.25.cloned.1.call-start = ((), (), s32[]{:S(2)}) async-start(), calls=%async_computation.18 | async-start | bytes 1572864 | tf_op jit(solution)/shard_map/while/body/eval_jaxpr/all_gather | solution.py:64
  687.9 192.1 %all-gather.23.cloned.1.call-start = ((), (), s32[]{:S(2)}) async-start(), calls=%async_computation.17 | async-start | bytes 5013504 | tf_op jit(solution)/shard_map/while/body/eval_jaxpr/all_gather | solution.py:191
  688.5 242.4 %reduce-scatter.16.cloned.1.call-start = ((), (), s32[]{:S(2)}) async-start(), calls=%async_computation.19 | async-start | bytes 3145728 | tf_op jit(solution)/shard_map/while/body/eval_jaxpr/reduce_scatter | solution.py:60
  720.5 217.5 %copy-start.25 = (f32[512]{0:T(512)}, f32[512]{0:T(512)S(1)}, u32[]{:S(2)}) copy-start(f32[512]{0:T(512)S(1)} %add_rsqrt_fusion.11) | copy-start | bytes 6148 | tf_op jit(solution)/shard_map/while
  900.4 62.2 %all-gather.27.cloned.1.call-start = ((), (), s32[]{:S(2)}) async-start(), calls=%async_computation.20 | async-start | bytes 1572864 | tf_op jit(solution)/shard_map/while/body/eval_jaxpr/all_gather | solution.py:64
  941.1 76.0 %reduce-scatter.20.cloned.1.call-start = ((), (), s32[]{:S(2)}) async-start(), calls=%async_computation.22 | async-start | bytes 3145728 | tf_op jit(solution)/shard_map/while/body/eval_jaxpr/reduce_scatter | solution.py:56
  948.9 83.9 %reduce-scatter.18.cloned.1.call-start = ((), (), s32[]{:S(2)}) async-start(), calls=%async_computation.21 | async-start | bytes 3145728 | tf_op jit(solution)/shard_map/while/body/eval_jaxpr/reduce_scatter | solution.py:60
  1042.7 81.8 %copy-start.33 = (f32[1024]{0:T(1024)}, f32[1024]{0:T(1024)S(1)}, u32[]{:S(2)}) copy-start(f32[1024]{0:T(1024)S(1)} %get-tuple-element.908) | copy-start | bytes 12292 | tf_op jit(solution)/shard_map/while
  1042.8 408.5 %copy-start.31 = (f32[512]{0:T(512)}, f32[512]{0:T(512)S(1)}, u32[]{:S(2)}) copy-start(f32[512]{0:T(512)S(1)} %get-tuple-element.921) | copy-start | bytes 6148 | tf_op jit(solution)/shard_map/while
  1042.8 40.8 %all-gather.13.cloned.1.call-start = ((), (), s32[]{:S(2)}) async-start(), calls=%async_computation.11 | async-start | bytes 1114112 | tf_op jit(solution)/shard_map/while/body/eval_jaxpr/all_gather | solution.py:140
  1043.5 79.5 %all-gather.15.cloned.1.call-start = ((), (), s32[]{:S(2)}) async-start(), calls=%async_computation.12 | async-start | bytes 1114112 | tf_op jit(solution)/shard_map/while/body/eval_jaxpr/all_gather | solution.py:141
  1044.1 117.9 %all-gather.19.cloned.1.call-start = ((), (), s32[]{:S(2)}) async-start(), calls=%async_computation.14 | async-start | bytes 1114112 | tf_op jit(solution)/shard_map/while/body/eval_jaxpr/all_gather | solution.py:142
  1044.7 151.5 %reduce-scatter.14.cloned.1.call-start = ((), (), s32[]{:S(2)}) async-start(), calls=%async_computation.15 | async-start | bytes 3145728 | tf_op jit(solution)/shard_map/while/body/eval_jaxpr/reduce_scatter | solution.py:56
  1165.3 66.6 %all-gather.21.cloned.1.call-start = ((), (), s32[]{:S(2)}) async-start(), calls=%async_computation.16 | async-start | bytes 3145728 | tf_op jit(solution)/shard_map/while/body/eval_jaxpr/all_gather | solution.py:170
  1198.6 117.2 %all-gather.17.cloned.1.call-start = ((), (), s32[]{:S(2)}) async-start(), calls=%async_computation.13 | async-start | bytes 10027008 | tf_op jit(solution)/shard_map/while/body/eval_jaxpr/all_gather | solution.py:143
  1199.2 138.2 %all-gather.25.cloned.1.call-start = ((), (), s32[]{:S(2)}) async-start(), calls=%async_computation.18 | async-start | bytes 1572864 | tf_op jit(solution)/shard_map/while/body/eval_jaxpr/all_gather | solution.py:64
  1201.1 192.3 %all-gather.23.cloned.1.call-start = ((), (), s32[]{:S(2)}) async-start(), calls=%async_computation.17 | async-start | bytes 5013504 | tf_op jit(solution)/shard_map/while/body/eval_jaxpr/all_gather | solution.py:191
  1201.9 242.4 %reduce-scatter.16.cloned.1.call-start = ((), (), s32[]{:S(2)}) async-start(), calls=%async_computation.19 | async-start | bytes 3145728 | tf_op jit(solution)/shard_map/while/body/eval_jaxpr/reduce_scatter | solution.py:60
  1233.7 217.6 %copy-start.25 = (f32[512]{0:T(512)}, f32[512]{0:T(512)S(1)}, u32[]{:S(2)}) copy-start(f32[512]{0:T(512)S(1)} %add_rsqrt_fusion.11) | copy-start | bytes 6148 | tf_op jit(solution)/shard_map/while
  1413.7 62.2 %all-gather.27.cloned.1.call-start = ((), (), s32[]{:S(2)}) async-start(), calls=%async_computation.20 | async-start | bytes 1572864 | tf_op jit(solution)/shard_map/while/body/eval_jaxpr/all_gather | solution.py:64
  1454.4 75.7 %reduce-scatter.20.cloned.1.call-start = ((), (), s32[]{:S(2)}) async-start(), calls=%async_computation.22 | async-start | bytes 3145728 | tf_op jit(solution)/shard_map/while/body/eval_jaxpr/reduce_scatter | solution.py:56
  1462.2 83.6 %reduce-scatter.18.cloned.1.call-start = ((), (), s32[]{:S(2)}) async-start(), calls=%async_computation.21 | async-start | bytes 3145728 | tf_op jit(solution)/shard_map/while/body/eval_jaxpr/reduce_scatter | solution.py:60
  1556.0 81.8 %copy-start.33 = (f32[1024]{0:T(1024)}, f32[1024]{0:T(1024)S(1)}, u32[]{:S(2)}) copy-start(f32[1024]{0:T(1024)S(1)} %get-tuple-element.908) | copy-start | bytes 12292 | tf_op jit(solution)/shard_map/while
  1556.0 408.5 %copy-start.31 = (f32[512]{0:T(512)}, f32[512]{0:T(512)S(1)}, u32[]{:S(2)}) copy-start(f32[512]{0:T(512)S(1)} %get-tuple-element.921) | copy-start | bytes 6148 | tf_op jit(solution)/shard_map/while
  1556.0 40.6 %all-gather.13.cloned.1.call-start = ((), (), s32[]{:S(2)}) async-start(), calls=%async_computation.11 | async-start | bytes 1114112 | tf_op jit(solution)/shard_map/while/body/eval_jaxpr/all_gather | solution.py:140
  1556.6 79.7 %all-gather.15.cloned.1.call-start = ((), (), s32[]{:S(2)}) async-start(), calls=%async_computation.12 | async-start | bytes 1114112 | tf_op jit(solution)/shard_map/while/body/eval_jaxpr/all_gather | solution.py:141
  1557.3 117.8 %all-gather.19.cloned.1.call-start = ((), (), s32[]{:S(2)}) async-start(), calls=%async_computation.14 | async-start | bytes 1114112 | tf_op jit(solution)/shard_map/while/body/eval_jaxpr/all_gather | solution.py:142
  1557.9 151.4 %reduce-scatter.14.cloned.1.call-start = ((), (), s32[]{:S(2)}) async-start(), calls=%async_computation.15 | async-start | bytes 3145728 | tf_op jit(solution)/shard_map/while/body/eval_jaxpr/reduce_scatter | solution.py:56
  1678.5 66.6 %all-gather.21.cloned.1.call-start = ((), (), s32[]{:S(2)}) async-start(), calls=%async_computation.16 | async-start | bytes 3145728 | tf_op jit(solution)/shard_map/while/body/eval_jaxpr/all_gather | solution.py:170
  1711.8 117.3 %all-gather.17.cloned.1.call-start = ((), (), s32[]{:S(2)}) async-start(), calls=%async_computation.13 | async-start | bytes 10027008 | tf_op jit(solution)/shard_map/while/body/eval_jaxpr/all_gather | solution.py:143
  1712.5 138.1 %all-gather.25.cloned.1.call-start = ((), (), s32[]{:S(2)}) async-start(), calls=%async_computation.18 | async-start | bytes 1572864 | tf_op jit(solution)/shard_map/while/body/eval_jaxpr/all_gather | solution.py:64
  1714.5 192.1 %all-gather.23.cloned.1.call-start = ((), (), s32[]{:S(2)}) async-start(), calls=%async_computation.17 | async-start | bytes 5013504 | tf_op jit(solution)/shard_map/while/body/eval_jaxpr/all_gather | solution.py:191
  1715.2 242.2 %reduce-scatter.16.cloned.1.call-start = ((), (), s32[]{:S(2)}) async-start(), calls=%async_computation.19 | async-start | bytes 3145728 | tf_op jit(solution)/shard_map/while/body/eval_jaxpr/reduce_scatter | solution.py:60
  1746.9 217.6 %copy-start.25 = (f32[512]{0:T(512)}, f32[512]{0:T(512)S(1)}, u32[]{:S(2)}) copy-start(f32[512]{0:T(512)S(1)} %add_rsqrt_fusion.11) | copy-start | bytes 6148 | tf_op jit(solution)/shard_map/while
  1926.9 62.2 %all-gather.27.cloned.1.call-start = ((), (), s32[]{:S(2)}) async-start(), calls=%async_computation.20 | async-start | bytes 1572864 | tf_op jit(solution)/shard_map/while/body/eval_jaxpr/all_gather | solution.py:64
  1967.6 76.3 %reduce-scatter.20.cloned.1.call-start = ((), (), s32[]{:S(2)}) async-start(), calls=%async_computation.22 | async-start | bytes 3145728 | tf_op jit(solution)/shard_map/while/body/eval_jaxpr/reduce_scatter | solution.py:56
  1975.4 84.1 %reduce-scatter.18.cloned.1.call-start = ((), (), s32[]{:S(2)}) async-start(), calls=%async_computation.21 | async-start | bytes 3145728 | tf_op jit(solution)/shard_map/while/body/eval_jaxpr/reduce_scatter | solution.py:60
  2072.6 82.1 %reduce-scatter.8.cloned.1.call-start = ((), (), s32[]{:S(2)}) async-start(), calls=%async_computation.7 | async-start | bytes 1114112 | tf_op jit(solution)/shard_map/reduce_scatter | solution.py:287
  2075.4 119.3 %reduce-scatter.10.cloned.1.call-start = ((), (), s32[]{:S(2)}) async-start(), calls=%async_computation.8 | async-start | bytes 1114112 | tf_op jit(solution)/shard_map/reduce_scatter | solution.py:296
  2078.0 320.3 %all-reduce.6.cloned.1.call-start = ((), (), s32[]{:S(2)}) async-start(), calls=%async_computation.10 | async-start | bytes 20971520
  2105.5 372.5 %reduce-scatter.12.cloned.1.call-start = ((), (), s32[]{:S(2)}) async-start(), calls=%async_computation.9 | async-start | bytes 5013504 | tf_op jit(solution)/shard_map/reduce_scatter | solution.py:305
  (180 other events, 1871.9 us)
Sparse Core Ops, SparseCore 0:
  18.0 40.6 all-gather.12
  61.4 36.8 all-gather.14
  100.5 36.8 all-gather.18
  140.8 30.7 reduce-scatter.13
  174.1 33.1 all-gather.20
  209.7 81.4 all-gather.16
  293.4 19.4 all-gather.24
  315.4 53.3 all-gather.22
  389.2 30.3 reduce-scatter.15
  429.9 21.3 all-gather.26
  453.5 31.8 reduce-scatter.19
  487.5 31.8 reduce-scatter.17
  532.4 37.9 all-gather.12
  573.0 36.8 all-gather.14
  611.9 36.8 all-gather.18
  652.2 30.7 reduce-scatter.13
  685.5 33.1 all-gather.20
  721.1 81.4 all-gather.16
  804.8 19.4 all-gather.24
  826.6 53.3 all-gather.22
  900.5 30.3 reduce-scatter.15
  941.2 21.2 all-gather.26
  964.8 31.8 reduce-scatter.19
  998.8 31.8 reduce-scatter.17
  1045.8 37.7 all-gather.12
  1086.1 36.8 all-gather.14
  1125.1 36.8 all-gather.18
  1165.4 30.7 reduce-scatter.13
  1198.7 33.1 all-gather.20
  1234.3 81.4 all-gather.16
  1317.9 19.4 all-gather.24
  1340.0 53.3 all-gather.22
  1413.8 30.3 reduce-scatter.15
  1454.5 21.3 all-gather.26
  1478.1 31.8 reduce-scatter.19
  1512.1 31.8 reduce-scatter.17
  1558.7 37.8 all-gather.12
  1599.3 36.8 all-gather.14
  1638.3 36.8 all-gather.18
  1678.6 30.7 reduce-scatter.13
  1711.9 33.1 all-gather.20
  1747.6 81.4 all-gather.16
  1831.1 19.4 all-gather.24
  1853.1 53.3 all-gather.22
  1927.0 30.3 reduce-scatter.15
  1967.7 21.2 all-gather.26
  1991.1 31.8 reduce-scatter.19
  2025.2 31.8 reduce-scatter.17
Sparse Core Ops, SparseCore 1:
  2077.2 56.9 reduce-scatter.7
  2138.2 56.4 reduce-scatter.9
  2198.4 199.9 all-reduce.5
  2402.7 75.2 reduce-scatter.11
where the time goes:
time: 2490 us
  waiting for transfers between devices  1700 us (68%)
  matrix products  411 us (17%)
  other arithmetic  156 us (6%)
  local copies, waits for them, and re-layouts  110 us (4%)
  blocking collectives  78.6 us (3%)
    all_gather x4, waiting for transfers between devices, micro(): lax.all_gather(w_gateup, 'dp', axis=0, tiled=True)  328 us
    all_gather x4, waiting for transfers between devices, micro(): lax.all_gather(w_down, 'dp', axis=1, tiled=True)  224 us
    unnamed x5, waiting for transfers between devices  202 us
    all_gather x4, waiting for transfers between devices, micro(): lax.all_gather(w_query, 'dp', axis=0, tiled=True)  147 us
    all_gather x4, waiting for transfers between devices, micro(): lax.all_gather(key_value_weight, 'dp', axis=0, tiled=True)  144 us
    reduce_scatter x8, waiting for transfers between devices, normed_grad(): return lax.psum_scatter(term, 'mp', scatter_dimension=1, tiled=True)  131 us
    all_gather x4, waiting for transfers between devices, micro(): resid_all = lax.all_gather(resid, 'mp', axis=1, tiled=True)  119 us
    reduce_scatter x8, waiting for transfers between devices, branch_sum(): return lax.psum_scatter(term, 'mp', scatter_dimension=1, tiled=True)  117 us
  transfers between devices with their start and end apart: 52, of which 44 were waited for; matrix products, arithmetic and copies ran while one was open for 20% of the time, Pallas kernels for 0%

commit v1 on v0

v1 whole, which is shorter than its diff:
```python
import jax
import jax.numpy as jnp
from jax import lax
from jax.sharding import PartitionSpec as P

HEAD_SIZE = 64
CHUNKS = 2

epsilon = 1e-05
rope_base = 1000000.0
f32 = jnp.float32
bf16 = jnp.bfloat16


def rotate_table(place):
    half = HEAD_SIZE // 2
    frequency = rope_base ** (-(jnp.arange(half, dtype=f32) * 2.0 / HEAD_SIZE))
    angle = place.astype(f32)[:, None] * frequency[None, :]
    return (jnp.cos(angle)[:, None, :], jnp.sin(angle)[:, None, :])


def rotate(value, cosine, sine):
    half = HEAD_SIZE // 2
    first, second = (value[..., :half], value[..., half:])
    return jnp.concatenate(
        [first * cosine - second * sine, second * cosine + first * sine], axis=-1
    )


def head_norm(value, gain):
    scale = lax.rsqrt(jnp.mean(value * value, axis=-1, keepdims=True) + epsilon)
    unit = value * scale
    return (unit * gain, unit, scale)


def head_norm_back(grad, unit, scale, gain):
    scaled = grad * gain
    inner = jnp.mean(unit * scaled, axis=-1, keepdims=True)
    return (scale * (scaled - unit * inner), jnp.sum(grad * unit, axis=(0, 1)))


def gather_rows(part):
    return lax.all_gather(part, "dp", axis=0, tiled=True)


def scatter_rows(total):
    return lax.psum_scatter(total, "dp", scatter_dimension=0, tiled=True).astype(f32)


def after(value, *earlier):
    return lax.optimization_barrier((value,) + earlier)


def shift(value, step):
    parts = lax.axis_size("mp")
    return lax.ppermute(value, "mp", [((i + step) % parts, i) for i in range(parts)])


def whole(own):
    parts = lax.axis_size("mp")
    index = lax.axis_index("mp")
    pieces = [own] + [shift(own, step) for step in range(1, parts)]
    placed = []
    for spot in range(parts):
        piece = pieces[spot]
        for holder in range(1, parts):
            piece = jnp.where(index == holder, pieces[(spot - holder) % parts], piece)
        placed.append(piece)
    return jnp.concatenate(placed, axis=1)


def row_sum(value):
    parts = lax.axis_size("mp")
    total = value
    for step in range(1, parts):
        total = total + shift(value, step)
    return total


def branch(value, rows):
    parts = lax.axis_size("mp")
    index = lax.axis_index("mp")
    width = rows.shape[0] // parts

    def term(owner, kind):
        piece = lax.dynamic_slice_in_dim(rows, owner * width, width, 0)
        return lax.dot_general(
            value, piece, (((1,), (1,)), ((), ())), preferred_element_type=f32
        ).astype(kind)

    got = []
    for step in range(1, parts):
        got.append(shift(term(lax.rem(index + parts - step, parts), bf16), step))
    total = term(index, f32)
    for piece in got:
        total = total + piece.astype(f32)
    return total


def over_tokens(left, right):
    left = jnp.concatenate(left, axis=0)
    right = jnp.concatenate(right, axis=0)
    return lax.dot_general(
        left, right, (((0,), (0,)), ((), ())), preferred_element_type=f32
    ).astype(bf16)


def score(query_rot, key_rot, segment):
    length, kv_heads = (key_rot.shape[0], key_rot.shape[1])
    order = jnp.arange(length)
    mask = (segment[:, None] == segment[None, :]) & (order[None, :] <= order[:, None])
    grouped = query_rot.reshape(length, kv_heads, -1, HEAD_SIZE)
    scores = jnp.einsum(
        "qhgd,khd->hgqk", grouped, key_rot, preferred_element_type=f32
    ) * HEAD_SIZE ** (-0.5)
    return jnp.where(mask, scores, -1e30)


def attend(scores, values):
    length = values.shape[0]
    top = jnp.max(scores, axis=-1, keepdims=True)
    expo = jnp.exp(scores - top)
    total = jnp.sum(expo, axis=-1, keepdims=True)
    weights = (expo / total).astype(bf16)
    attended = jnp.einsum("hgqk,khd->qhgd", weights, values, preferred_element_type=f32)
    return (attended.reshape(length, -1).astype(bf16), weights)


def attend_back(query_rot, key_rot, values, weights, attended, grad_out):
    length, kv_heads = (key_rot.shape[0], key_rot.shape[1])
    shape = (length, kv_heads, -1, HEAD_SIZE)
    grouped = query_rot.reshape(shape)
    grad_grouped = grad_out.reshape(shape)
    inner = jnp.sum(attended.reshape(shape).astype(f32) * grad_grouped.astype(f32), axis=-1)
    inner = inner.transpose(1, 2, 0)[..., None]
    grad_probs = jnp.einsum("qhgd,khd->hgqk", grad_grouped, values, preferred_element_type=f32)
    grad_scores = (weights.astype(f32) * (grad_probs - inner)).astype(bf16)
    grad_values = jnp.einsum("hgqk,qhgd->khd", weights, grad_grouped, preferred_element_type=f32)
    grad_query = jnp.einsum(
        "hgqk,khd->qhgd", grad_scores, key_rot, preferred_element_type=f32
    ) * HEAD_SIZE ** (-0.5)
    grad_key = jnp.einsum(
        "hgqk,qhgd->khd", grad_scores, grouped, preferred_element_type=f32
    ) * HEAD_SIZE ** (-0.5)
    return (grad_query.reshape(length, -1, HEAD_SIZE), grad_key, grad_values)


def body(
    tokens,
    cotangent,
    segment_ids,
    positions,
    attn_gain,
    w_query,
    key_value_weight,
    w_out,
    qk_gain,
    ffn_gain,
    w_gateup,
    w_down,
):
    parts = lax.axis_size("mp")
    sequences, length, model = tokens.shape
    width = model // parts
    offset = lax.axis_index("mp") * width
    rows, kv_heads = key_value_weight.shape[:2]
    ff = w_gateup.shape[2]
    cols = w_query.shape[1]
    kv_cols = kv_heads * 2 * HEAD_SIZE
    gain_first = attn_gain.astype(f32)
    gain_second = ffn_gain.astype(f32)
    first_part = lax.dynamic_slice_in_dim(gain_first, offset, width)
    second_part = lax.dynamic_slice_in_dim(gain_second, offset, width)
    query_gain = qk_gain[0].astype(f32)
    key_gain = qk_gain[1].astype(f32)

    attn_rows = gather_rows(
        jnp.concatenate([w_query, key_value_weight.reshape(rows, kv_cols), w_out.T], axis=1)
    )
    gateup_rows = gather_rows(w_gateup.reshape(rows, 2 * ff))
    down_rows = gather_rows(w_down.T)

    chunks = CHUNKS if sequences % CHUNKS == 0 else 1
    each = sequences // chunks
    count = each * length
    run = range(chunks)

    def cut(value, i):
        return value[i * each : (i + 1) * each]

    def flat(value, i):
        return cut(value, i).reshape((count,) + value.shape[2:])

    grad_own = [flat(cotangent, i) for i in run]
    grad_whole = [whole(grad_own[i]) for i in run]
    attn_rows, *grad_whole = after(attn_rows, *grad_whole)
    qkv_w = attn_rows[:, : cols + kv_cols]
    out_rows = attn_rows[:, cols + kv_cols :]
    normed_first, own_unit, scale_first, own = [], [], [], []
    heads = []
    attended, kept, resid = [], [], []
    for i in run:
        block = flat(tokens, i).astype(f32)
        scale = lax.rsqrt(jnp.mean(block * block, axis=-1, keepdims=True) + epsilon)
        normed_first.append((block * scale * gain_first).astype(bf16))
        part = lax.dynamic_slice_in_dim(flat(tokens, i), offset, width, 1).astype(f32)
        own.append(part)
        own_unit.append(part * scale)
        scale_first.append(scale)
        raw = jnp.dot(normed_first[i], qkv_w, preferred_element_type=f32)
        query_raw = raw[:, :cols].reshape(count, -1, HEAD_SIZE)
        keyval_raw = raw[:, cols:].reshape(count, kv_heads, 2 * HEAD_SIZE)
        cosine, sine = rotate_table(cut(positions, i).reshape(count))
        query_normed, query_unit, query_scale = head_norm(query_raw, query_gain)
        key_normed, key_unit, key_scale = head_norm(keyval_raw[..., :HEAD_SIZE], key_gain)
        shape = (each, length, -1, HEAD_SIZE)
        query_rot = rotate(query_normed, cosine, sine).astype(bf16).reshape(shape)
        key_rot = rotate(key_normed, cosine, sine).astype(bf16).reshape(shape)
        values = keyval_raw[..., HEAD_SIZE:].astype(bf16).reshape(shape)
        scores = jax.vmap(score)(query_rot, key_rot, cut(segment_ids, i))
        if i > 0:
            scores, resid[i - 1] = after(scores, resid[i - 1])
        out, weights = jax.vmap(attend)(scores, values)
        attended.append(out.reshape(count, cols))
        kept.append((query_rot, key_rot, values, weights, out))
        heads.append((cosine, sine, query_unit, query_scale, key_unit, key_scale))
        resid.append(own[i] + branch(attended[i], out_rows))

    normed_second, unit_second, scale_second = [], [], []
    hidden, gates, mixed = [], [], []
    for i in run:
        resid_all = whole(resid[i].astype(bf16)).astype(f32)
        square = row_sum(jnp.sum(resid[i] * resid[i], axis=-1))[:, None]
        scale = lax.rsqrt(square / model + epsilon)
        scale_second.append(scale)
        normed_second.append((resid_all * scale * gain_second).astype(bf16))
        unit_second.append(resid[i] * scale)
        gate = jnp.dot(normed_second[i], gateup_rows[:, :ff], preferred_element_type=f32)
        if i + 1 < chunks:
            gate, resid[i + 1] = after(gate, resid[i + 1])
        upper = jnp.dot(normed_second[i], gateup_rows[:, ff:], preferred_element_type=f32)
        sigmoid_gate = jax.nn.sigmoid(gate)
        hidden.append((gate * sigmoid_gate * upper).astype(bf16))
        gates.append((gate, upper, sigmoid_gate))
    for i in run:
        mixed.append((resid[i] + branch(hidden[i], down_rows)).astype(bf16))

    down_total = over_tokens(grad_whole, hidden)
    grad_whole[-1], down_total = after(grad_whole[-1], down_total)
    down_sum = scatter_rows(down_total).T
    grad_gateup, grad_second = [], []
    for i in run:
        gate, upper, sigmoid_gate = gates[i]
        grad_hidden = jnp.dot(grad_whole[i], down_rows, preferred_element_type=f32)
        grad_gate = grad_hidden * upper * sigmoid_gate * (1.0 + gate * (1.0 - sigmoid_gate))
        grad_upper = grad_hidden * gate * sigmoid_gate
        grad_gateup.append(
            jnp.concatenate([grad_gate.astype(bf16), grad_upper.astype(bf16)], axis=-1)
        )
        grad_second.append(branch(grad_gateup[i], gateup_rows))
    gateup_total = over_tokens(normed_second, grad_gateup)
    grad_second[-1], gateup_total = after(grad_second[-1], gateup_total)
    gateup_sum = scatter_rows(gateup_total).reshape(rows, 2, ff)

    def slice_norm_back(grad, unit, scale, gain):
        scaled = grad * gain
        inner = row_sum(jnp.sum(unit * scaled, axis=-1))[:, None]
        return (scale * (scaled - unit * (inner / model)), jnp.sum(grad * unit, axis=0))

    grad_resid, grad_branch, second_gain = [], [], 0.0
    for i in run:
        back, gain = slice_norm_back(
            grad_second[i], unit_second[i], scale_second[i], second_part
        )
        second_gain = second_gain + gain
        grad_resid.append(back + grad_own[i].astype(f32))
        grad_branch.append(whole(grad_resid[i].astype(bf16)))
    out_total = over_tokens(grad_branch, attended)
    grad_branch[-1], out_total = after(grad_branch[-1], out_total)
    out_sum = scatter_rows(out_total).T

    grad_qkv, grad_input = [], []
    first_gain = pair_gain = 0.0
    for i in run:
        cosine, sine, query_unit, query_scale, key_unit, key_scale = heads[i]
        grad_attended = jnp.dot(
            grad_branch[i], out_rows, preferred_element_type=f32
        ).astype(bf16)
        grads = jax.vmap(attend_back)(*kept[i], grad_attended.reshape(each, length, cols))
        grad_query, grad_key, grad_values = (
            value.reshape(count, -1, HEAD_SIZE) for value in grads
        )
        query_raw_grad, query_gain_grad = head_norm_back(
            rotate(grad_query, cosine, -sine), query_unit, query_scale, query_gain
        )
        key_raw_grad, key_gain_grad = head_norm_back(
            rotate(grad_key, cosine, -sine), key_unit, key_scale, key_gain
        )
        keyval_raw_grad = jnp.concatenate([key_raw_grad, grad_values], axis=-1)
        grad_qkv.append(
            jnp.concatenate(
                [
                    query_raw_grad.reshape(count, -1).astype(bf16),
                    keyval_raw_grad.reshape(count, -1).astype(bf16),
                ],
                axis=-1,
            )
        )
        grad_first = branch(grad_qkv[i], qkv_w)
        back, gain = slice_norm_back(grad_first, own_unit[i], scale_first[i], first_part)
        first_gain = first_gain + gain
        pair_gain = pair_gain + jnp.stack([query_gain_grad, key_gain_grad])
        grad_input.append(back + grad_resid[i])
    qkv_sum = scatter_rows(over_tokens(normed_first, grad_qkv))

    gains = jnp.zeros((2 * model,), f32)
    gains = lax.dynamic_update_slice_in_dim(gains, first_gain, offset, 0)
    gains = lax.dynamic_update_slice_in_dim(gains, second_gain, model + offset, 0)
    gains = lax.psum(jnp.concatenate([gains, pair_gain.reshape(-1)]), ("dp", "mp"))

    def joined(pieces):
        return jnp.concatenate(pieces, axis=0).reshape(sequences, length, width)

    return (
        joined(mixed),
        joined(grad_input),
        gains[:model],
        qkv_sum[:, :cols],
        qkv_sum[:, cols:].reshape(rows, kv_heads, 2 * HEAD_SIZE),
        out_sum,
        gains[2 * model :].reshape(2, HEAD_SIZE),
        gains[model : 2 * model],
        gateup_sum,
        down_sum,
    )


def solution(mesh):
    placed = (
        P("dp", None, None),
        P("dp", None, "mp"),
        P("dp", None),
        P("dp", None),
        P(),
        P("dp", "mp"),
        P("dp", "mp", None),
        P("mp", "dp"),
        P(),
        P(),
        P("dp", None, "mp"),
        P("mp", "dp"),
    )
    return jax.shard_map(
        body,
        mesh=mesh,
        in_specs=placed,
        out_specs=(
            P("dp", None, "mp"),
            P("dp", None, "mp"),
            P(),
            P("dp", "mp"),
            P("dp", "mp", None),
            P("mp", "dp"),
            P(),
            P(),
            P("dp", None, "mp"),
            P("mp", "dp"),
        ),
        check_vma=False,
    )
```

time: 2490 us -> 830 us (0.33)
  waiting for transfers between devices: 1700 us -> 276 us
  matrix products: 411 us -> 272 us
  other arithmetic: 156 us -> 110 us
  blocking collectives: 78.6 us -> 39.8 us
    all_gather x32 -> x3, waiting for transfers between devices: 1130 us -> 0.02 us  [gather_rows(): return lax.all_gather(part, 'dp', axis=0, tiled=True)]
    reduce_scatter x19 -> x4, waiting for transfers between devices: 362 us -> 146 us  [scatter_rows(): lax.psum_scatter(total, 'dp', scatter_dimension=0, tiled=True).astype(f32)]
    unnamed x5 -> x7, waiting for transfers between devices: 202 us -> 1.77 us
    dot_general x68 -> x33, matrix products: 374 us -> 230 us  [the longest x16 80.5 us: term(): lax.dot_general(value, piece, (((1,), (1,)), ((), ())), preferred_element...]
    ppermute x0 -> x20, waiting for transfers between devices: none -> 128 us  [shift(): lax.ppermute(value, 'mp', [((i + step) % parts, i) for i in range(parts)])]
    while x382 -> x0, local copies, waits for them, and re-layouts: 71.4 us -> none
    psum x9 -> x1, blocking collectives: 78.6 us -> 39.8 us  [body(): lax.psum(jnp.concatenate([gains, pair_gain.reshape(-1)]), ('dp', 'mp'))]
    convert_element_type x31 -> x10, other arithmetic: 61.3 us -> 29.6 us  [the longest x2 14.6 us: attend(): weights = (expo / total).astype(bf16)]
  transfers between devices with their start and end apart: 52 -> 27, of which waited for: 44 -> 11; matrix products, arithmetic and copies ran while one was open for 20% -> 45% of each run, Pallas kernels for 0% -> 0%
where the time goes in v1:
time: 830 us; the launch traced here: 826 us
  waiting for transfers between devices  276 us (33%)
  matrix products  272 us (33%)
  other arithmetic  110 us (13%)
  local copies, waits for them, and re-layouts  88.1 us (11%)
  blocking collectives  39.8 us (5%)
  starting transfers between devices  22.7 us (3%)
  between operations  16.4 us (2%)
    reduce_scatter x4, waiting for transfers between devices, scatter_rows(): lax.psum_scatter(total, 'dp', scatter_dimension=0, tiled=True).astype(f32)  146 us
    ppermute x20, waiting for transfers between devices, shift(): lax.ppermute(value, 'mp', [((i + step) % parts, i) for i in range(parts)])  128 us
    dot_general x16, matrix products, term(): lax.dot_general(value, piece, (((1,), (1,)), ((), ())), preferred_element...  80.5 us
    dot_general x4, matrix products, over_tokens(): lax.dot_general(left, right, (((0,), (0,)), ((), ())), preferred_element_...  53.9 us
    psum x1, blocking collectives, body(): lax.psum(jnp.concatenate([gains, pair_gain.reshape(-1)]), ('dp', 'mp'))  39.8 us
    dot_general x2, matrix products, body(): jnp.dot(normed_second[i], gateup_rows[:, ff:], preferred_element_type=f32)  28.2 us
    unnamed x298, local copies, waits for them, and re-layouts  24.1 us
    dot_general x2, matrix products, body(): grad_hidden = jnp.dot(grad_whole[i], down_rows, preferred_element_type=f32)  23.4 us
  transfers between devices with their start and end apart: 27, of which 11 were waited for; matrix products, arithmetic and copies ran while one was open for 45% of the time, Pallas kernels for 0%

profile of v1, /device:TPU:0, one launch (start us, length us, event | category | flops | bytes accessed | tf_op | source)
XLA Modules:
  0.0 825.8 jit_solution(12978735913684752141)
XLA Ops:
  10.5 2.7 fusion.221
  13.3 2.9 collective-permute-start.1
  17.2 3.3 multiply_reduce_fusion
  28.8 3.9 multiply_convert_fusion.8
  32.7 7.6 collective-permute-done.1
  41.7 20.3 %collective-permute-done = bf16[1024,512]{1,0:T(8,128)(2,1)} collective-permute-done((bf16[1024,512]{1,0:T(8,128)(2,1)}, bf16[1024,512]{1,0:T(8,128)(2,1)}, u32[]{:S(2)}, u32[]{:S(2)}) %collective-permute-start) | collective-permute-done | bytes 1048608 | tf_op jit(solution)/shard_map/ppermute | solution.py:56
  63.6 2.6 pad_maximum_fusion.7
  68.6 4.1 fusion.216
  74.4 2.5 copy-done.62
  87.2 2.7 slice.303
  96.3 11.0 %fusion.225 = (f32[2,4,2,512]{3,2,1,0:T(2,128)S(1)}, f32[2,4,2,512,512]{3,4,2,1,0:T(8,128)}) fusion(pred[2,512,512]{1,2,0:T(8,128)(4,1)} %get-tuple-element.101, bf16[2,512,4,2,64]{1,4,3,2,0:T(8,128)(2,1)S(1)} %copy_dynamic-update-slice_fusion, bf16[2,512,4,32]{1,3,2,0:T(8,128)(2,1)} %bitcast.334, bf16[2,512,4,32]{1,3,2,0:T(8,128)(2,1)} %bitcast.336), kind=kOutput, calls=%fused_computation.362 | convolution fusion | flops 554697216 | bytes 18907136 | tf_op jit(solution)/shard_map/vmap()/sub | solution.py:122
  107.4 7.3 divide_convert_fusion.1
  130.8 8.4 %bitcast_select_fusion.1 = f32[2,4,2,512,512]{3,4,2,1,0:T(8,128)} fusion(pred[2,512,512]{1,2,0:T(8,128)(4,1)S(1)} %copy-done.38, bf16[2,512,4,2,64]{1,4,3,2,0:T(8,128)(2,1)S(1)} %copy_dynamic-update-slice_fusion.2, bf16[2,512,4,32]{1,3,2,0:T(8,128)(2,1)S(1)} %bitcast.326, bf16[2,512,4,32]{1,3,2,0:T(8,128)(2,1)S(1)} %bitcast.328), kind=kOutput, calls=%fused_computation.17 | convolution fusion | flops 546308096 | bytes 18874368 | tf_op jit(solution)/shard_map/vmap(qhgd,khd->hgqk)/dot_general | solution.py:113
  139.2 6.3 collective-permute-done.2
  150.7 19.2 %fusion.226 = (f32[2,4,2,512]{3,2,1,0:T(2,128)S(1)}, f32[2,4,2,512,512]{3,4,2,1,0:T(8,128)}) fusion(f32[2,4,2,512,512]{3,4,2,1,0:T(8,128)} %bitcast_select_fusion.1), kind=kOutput, calls=%fused_computation.363 | output fusion | flops 8389119 | bytes 33587200 | tf_op jit(solution)/shard_map/vmap()/sub | solution.py:122
  169.9 7.3 divide_convert_fusion
  185.4 20.5 %collective-permute-done.4 = f32[1024]{0:T(1024)S(1)} collective-permute-done((f32[1024]{0:T(1024)S(1)}, f32[1024]{0:T(1024)S(1)}, u32[]{:S(2)}, u32[]{:S(2)}) %collective-permute-start.4) | collective-permute-done | bytes 4128 | tf_op jit(solution)/shard_map/ppermute | solution.py:56
  209.1 10.7 %fusion.227 = f32[1024,2304]{1,0:T(8,128)} fusion(bf16[1024,1024]{1,0:T(8,128)(2,1)} %get-tuple-element.28, bf16[1024,2304]{1,0:T(8,128)(2,1)} %all-gather.8.cloned.1.call-done), kind=kOutput, calls=%fused_computation.364 | convolution fusion | flops 4831838208 | bytes 16252928 | tf_op jit(solution)/shard_map/dot_general | solution.py:254
  219.8 10.3 %fusion.63 = f32[1024,2304]{1,0:T(8,128)} fusion(bf16[1024,1024]{1,0:T(8,128)(2,1)} %multiply_convert_fusion.7, bf16[1024,4608]{1,0:T(8,128)(2,1)} %all-gather.6.cloned.1.call-done), kind=kOutput, calls=%fused_computation.84 | convolution fusion | flops 4831838208 | bytes 16252928 | tf_op jit(solution)/shard_map/dot_general | solution.py:238
  232.4 16.0 %multiply_convert_fusion.3 = (bf16[1024,2304]{1,0:T(8,128)(2,1)S(1)}, bf16[1024,2304]{1,0:T(8,128)(2,1)}, bf16[1024,2304]{1,0:T(8,128)(2,1)}) fusion(f32[1024,2304]{1,0:T(8,128)} %fusion.63, f32[1024,2304]{1,0:T(8,128)} %fusion.227, bf16[1024,1024]{1,0:T(8,128)(2,1)S(1)} %copy-done.74, bf16[1024,4608]{1,0:T(8,128)(2,1)} %all-gather.6.cloned.1.call-done), kind=kOutput, calls=%fused_computation.33 | convolution fusion | flops 4869586944 | bytes 39845888 | tf_op jit(solution)/shard_map/dot_general | solution.py:241
  250.6 9.3 %fusion.118 = bf16[1024,512]{1,0:T(8,128)(2,1)} fusion(bf16[1024,4608]{1,0:T(8,128)(2,1)} %all-gather.6.cloned.1.call-done, s32[]{:T(128)S(6)} %select_n.97, bf16[1024,2304]{1,0:T(8,128)(2,1)} %get-tuple-element.56, bf16[1024,2304]{1,0:T(8,128)(2,1)S(1)} %get-tuple-element.54), kind=kOutput, calls=%fused_computation.178 | convolution fusion | flops 4851236864 | bytes 15204356 | tf_op jit(solution)/shard_map/dot_general | solution.py:87
  261.5 10.6 %fusion.61 = f32[1024,2304]{1,0:T(8,128)} fusion(bf16[1024,1024]{1,0:T(8,128)(2,1)S(1)} %multiply_convert_fusion.6, bf16[1024,4608]{1,0:T(8,128)(2,1)} %all-gather.6.cloned.1.call-done), kind=kOutput, calls=%fused_computation.82 | convolution fusion | flops 4831838208 | bytes 16252928 | tf_op jit(solution)/shard_map/dot_general | solution.py:238
  272.2 12.2 %multiply_convert_fusion.4 = (bf16[1024,2304]{1,0:T(8,128)(2,1)}, f32[1024,2304]{1,0:T(8,128)}) fusion(f32[1024,2304]{1,0:T(8,128)} %fusion.61, bf16[1024,1024]{1,0:T(8,128)(2,1)S(1)} %multiply_convert_fusion.6, bf16[1024,4608]{1,0:T(8,128)(2,1)} %all-gather.6.cloned.1.call-done), kind=kOutput, calls=%fused_computation.34 | convolution fusion | flops 4845993984 | bytes 30408704 | tf_op jit(solution)/shard_map/dot_general | solution.py:241
  284.4 13.3 %fusion.29 = bf16[1024,2304]{1,0:T(8,128)(2,1)} fusion(bf16[1024,2304]{1,0:T(8,128)(2,1)} %get-tuple-element.136, bf16[1024,2304]{1,0:T(8,128)(2,1)S(1)} %bitcast.370, bf16[1024,1024]{1,0:T(8,128)(2,1)S(1)} %copy-done.81, bf16[1024,1024]{1,0:T(8,128)(2,1)S(1)} %copy-done.82), kind=kOutput, calls=%fused_computation.45 | convolution fusion | flops 9693298688 | bytes 18350080 | tf_op jit(solution)/shard_map/dot_general | solution.py:103
  297.7 12.7 %multiply_convert_fusion.1 = (bf16[1024,2304]{1,0:T(8,128)(2,1)S(1)}, bf16[1024,2304]{1,0:T(8,128)(2,1)S(1)}) fusion(f32[1024,2304]{1,0:T(8,128)} %fusion.61, f32[1024,2304]{1,0:T(8,128)} %get-tuple-element.137, bf16[1024,1024]{1,0:T(8,128)(2,1)S(1)} %copy-done.81, bf16[1024,2304]{1,0:T(8,128)(2,1)} %all-gather.8.cloned.1.call-done), kind=kOutput, calls=%fused_computation.31 | convolution fusion | flops 4862509056 | bytes 35127296 | tf_op jit(solution)/shard_map/dot_general | solution.py:254
  310.5 11.7 %fusion.121 = bf16[1024,512]{1,0:T(8,128)(2,1)} fusion(bf16[1024,4608]{1,0:T(8,128)(2,1)} %all-gather.6.cloned.1.call-done, s32[]{:T(128)S(6)} %select_n.97, bf16[1024,2304]{1,0:T(8,128)(2,1)S(1)} %get-tuple-element.58, bf16[1024,2304]{1,0:T(8,128)(2,1)S(1)} %get-tuple-element.57), kind=kOutput, calls=%fused_computation.179 | convolution fusion | flops 4851236864 | bytes 15204356 | tf_op jit(solution)/shard_map/dot_general | solution.py:87
  323.4 11.4 %multiply_reduce_fusion.3 = (f32[512]{0:T(512)}, f32[1024]{0:T(1024)S(1)}, f32[1024,512]{1,0:T(8,128)}) fusion(f32[1024,512]{1,0:T(8,128)S(1)} %copy-done.18, f32[1024]{0:T(1024)S(1)} %copy-done.117, bf16[1024,512]{1,0:T(8,128)(2,1)S(1)} %collective-permute-done.10, f32[512]{0:T(512)S(1)} %copy-done.118, ...), kind=kOutput, calls=%fused_computation.142 | convolution fusion | flops 4854905344 | bytes 19410948 | tf_op jit(solution)/shard_map/dot_general | solution.py:87
  335.7 31.4 %fusion.15 = bf16[1024,4608]{1,0:T(8,128)(2,1)} fusion(bf16[1024,2304]{1,0:T(8,128)(2,1)} %copy-done.134, bf16[1024,2304]{1,0:T(8,128)(2,1)} %copy-done.133, bf16[1024,2304]{1,0:T(8,128)(2,1)} %get-tuple-element.56, bf16[1024,2304]{1,0:T(8,128)(2,1)} %copy-done.135, bf16[1024,1024]{1,0:T(8,128)(2,1)} %copy-done.78, bf16[1024,1024]{1,0:T(8,128)(2,1)S(1)} %copy-done.75), kind=kOutput, calls=%fused_computation.23 | convolution fusion | flops 19415957504 | bytes 32505856 | tf_op jit(solution)/shard_map/dot_general | solution.py:103
  367.2 9.4 %convert_add_fusion.4 = f32[1024,512]{1,0:T(8,128)S(1)} fusion(bf16[1024,512]{1,0:T(8,128)(2,1)} %collective-permute-done.15, bf16[1024,4608]{1,0:T(8,128)(2,1)} %all-gather.6.cloned.1.call-done, s32[]{:T(128)S(6)} %select_n.95, bf16[1024,2304]{1,0:T(8,128)(2,1)} %copy-done.134, bf16[1024,2304]{1,0:T(8,128)(2,1)} %copy-done.133), kind=kOutput, calls=%fused_computation.149 | convolution fusion | flops 4851761152 | bytes 17301508 | tf_op jit(solution)/shard_map/dot_general | solution.py:87
  376.6 4.9 fusion.219
  383.6 18.8 %collective-permute-done.16 = f32[1024]{0:T(1024)S(1)} collective-permute-done((f32[1024]{0:T(1024)S(1)}, f32[1024]{0:T(1024)S(1)}, u32[]{:S(2)}, u32[]{:S(2)}) %collective-permute-start.16) | collective-permute-done | bytes 4128 | tf_op jit(solution)/shard_map/ppermute | solution.py:56
  402.4 3.3 fusion.218
  414.6 4.8 copy.82
  421.1 6.9 fusion.148
  427.9 4.9 fusion.13
  432.8 2.6 fusion.138
  437.0 3.0 copy.85
  440.0 4.3 reshape.471
  452.9 3.4 fusion.113
  462.3 4.6 copy.93
  468.6 5.7 fusion.11
  474.3 2.6 multiply_bitcast_fusion
  477.0 3.6 fusion.136
  480.6 3.4 fusion.147
  484.0 2.9 copy.96
  487.0 4.1 reshape.474
  493.9 5.0 multiply_reduce_fusion.7
  500.5 2.7 multiply_reduce_fusion.14
  509.9 5.9 fusion.108
  517.2 6.8 fusion.124
  526.5 6.5 fusion.127
  534.5 15.9 %collective-permute-done.6 = bf16[1024,512]{1,0:T(8,128)(2,1)} collective-permute-done((bf16[1024,512]{1,0:T(8,128)(2,1)}, bf16[1024,512]{1,0:T(8,128)(2,1)}, u32[]{:S(2)}, u32[]{:S(2)}) %collective-permute-start.6) | collective-permute-done | bytes 1048608 | tf_op jit(solution)/shard_map/ppermute | solution.py:56
  550.4 5.9 add_convert_fusion.1
  563.0 9.8 %collective-permute-done.9 = bf16[1024,512]{1,0:T(8,128)(2,1)S(1)} collective-permute-done((bf16[1024,512]{1,0:T(8,128)(2,1)S(1)}, bf16[1024,512]{1,0:T(8,128)(2,1)S(1)}, u32[]{:S(2)}, u32[]{:S(2)}) %collective-permute-start.9) | collective-permute-done | bytes 1048608 | tf_op jit(solution)/shard_map/ppermute | solution.py:56
  572.8 2.7 add_convert_fusion
  577.3 18.1 %collective-permute-done.13 = bf16[1024,512]{1,0:T(8,128)(2,1)} collective-permute-done((bf16[1024,512]{1,0:T(8,128)(2,1)}, bf16[1024,512]{1,0:T(8,128)(2,1)}, u32[]{:S(2)}, u32[]{:S(2)}) %collective-permute-start.13) | collective-permute-done | bytes 1048608 | tf_op jit(solution)/shard_map/ppermute | solution.py:56
  595.3 4.1 fusion.79
  600.1 11.1 %collective-permute-done.18 = bf16[1024,512]{1,0:T(8,128)(2,1)} collective-permute-done((bf16[1024,512]{1,0:T(8,128)(2,1)}, bf16[1024,512]{1,0:T(8,128)(2,1)}, u32[]{:S(2)}, u32[]{:S(2)}) %collective-permute-start.18) | collective-permute-done | bytes 1048608 | tf_op jit(solution)/shard_map/ppermute | solution.py:56
  611.2 2.8 convert_add_fusion.2
  617.2 39.8 %psum.7 = f32[2176]{0:T(1024)S(1)} all-reduce(f32[2176]{0:T(1024)S(1)} %pad_maximum_fusion.32), channel_id=1, replica_groups=mesh['dp'=16,'mp'=2] {'dp','mp'}, use_global_device_ids=true, to_apply=%region_32.33 | all-reduce | flops 2176 | bytes 17408 | tf_op jit(solution)/shard_map/psum | solution.py:319
  658.3 3.3 fusion.83
  667.8 33.1 %reduce-scatter.11.cloned.1.call-done = bf16[64,2304]{1,0:T(8,128)(2,1)} async-done(((bf16[1024,2304]{1,0:T(8,128)(2,1)}), bf16[64,2304]{1,0:T(8,128)(2,1)}) %reduce-scatter.11.cloned.1.call-update) | async-done | bytes 294928 | tf_op jit(solution)/shard_map/reduce_scatter | solution.py:47
  702.6 113.2 %reduce-scatter.9.cloned.1.call-done = bf16[64,4608]{1,0:T(8,128)(2,1)} async-done(((bf16[1024,4608]{1,0:T(8,128)(2,1)}), bf16[64,4608]{1,0:T(8,128)(2,1)}) %reduce-scatter.9.cloned.1.call-update) | async-done | bytes 589840 | tf_op jit(solution)/shard_map/reduce_scatter | solution.py:47
  815.9 2.8 reshape.485
  (470 shorter events, 144.5 us)
Async XLA Ops:
  7.2 59.1 %all-gather.4.cloned.1.call-start = ((), (), s32[]{:S(2)}) async-start(), calls=%async_computation.4 | async-start | bytes 3342336 | tf_op jit(solution)/shard_map/all_gather | solution.py:43
  9.7 199.4 %all-gather.8.cloned.1.call-start = ((), (), s32[]{:S(2)}) async-start(), calls=%async_computation.6 | async-start | bytes 5013504 | tf_op jit(solution)/shard_map/all_gather | solution.py:43
  10.5 209.3 %all-gather.6.cloned.1.call-start = ((), (), s32[]{:S(2)}) async-start(), calls=%async_computation.5 | async-start | bytes 10027008 | tf_op jit(solution)/shard_map/all_gather | solution.py:43
  13.3 27.0 %copy-start.24 = (bf16[2,512,512]{2,1,0:T(8,128)(2,1)}, bf16[2,512,512]{2,1,0:T(8,128)(2,1)S(1)}, u32[]{:S(2)}) copy-start(bf16[2,512,512]{2,1,0:T(8,128)(2,1)S(1)} %get-tuple-element.89) | copy-start | bytes 3145732
  13.3 27.0 %collective-permute-start.1 = (bf16[1024,512]{1,0:T(8,128)(2,1)S(1)}, bf16[1024,512]{1,0:T(8,128)(2,1)}, u32[]{:S(2)}, u32[]{:S(2)}) collective-permute-start(bf16[1024,512]{1,0:T(8,128)(2,1)S(1)} %bitcast.310), channel_id=1, source_target_pairs={{1,0},{0,1},{3,2},{2,3},{5,4},{4,5},{7,6},{6,7},{9,8},{8,9},{11,10... | collective-permute-start | bytes 3145736 | tf_op jit(solution)/shard_map/ppermute | solution.py:56
  16.2 45.7 %collective-permute-start = (bf16[1024,512]{1,0:T(8,128)(2,1)}, bf16[1024,512]{1,0:T(8,128)(2,1)}, u32[]{:S(2)}, u32[]{:S(2)}) collective-permute-start(bf16[1024,512]{1,0:T(8,128)(2,1)} %bitcast.2), channel_id=1, source_target_pairs={{1,0},{0,1},{3,2},{2,3},{5,4},{4,5},{7,6},{6,7},{9,8},{8,9},{11,10... | collective-permute-start | bytes 3145736 | tf_op jit(solution)/shard_map/ppermute | solution.py:56
  17.1 646.9 %reduce-scatter.7.cloned.1.call-start = ((), (), s32[]{:S(2)}) async-start(), calls=%async_computation.8 | async-start | bytes 1114112 | tf_op jit(solution)/shard_map/reduce_scatter | solution.py:47
  28.8 63.1 %copy-start.60 = (f32[1024,32]{0,1:T(8,128)}, f32[1024,32]{0,1:T(8,128)S(1)}, u32[]{:S(2)}) copy-start(f32[1024,32]{0,1:T(8,128)S(1)} %get-tuple-element.112) | copy-start | bytes 393220
  28.8 94.5 %copy-start.58 = (f32[1024,32]{0,1:T(8,128)}, f32[1024,32]{0,1:T(8,128)S(1)}, u32[]{:S(2)}) copy-start(f32[1024,32]{0,1:T(8,128)S(1)} %get-tuple-element.123) | copy-start | bytes 393220
  79.4 12.0 %copy-start.12 = (f32[1024,512]{0,1:T(8,128)}, f32[1024,512]{0,1:T(8,128)S(1)}, u32[]{:S(2)}) copy-start(f32[1024,512]{0,1:T(8,128)S(1)} %slice.193) | copy-start | bytes 6291460
  94.9 19.8 %copy-start.40 = (bf16[2,512,4,64]{1,0,3,2:T(2,128)(2,1)}, bf16[2,512,4,64]{1,0,3,2:T(2,128)(2,1)S(1)}, u32[]{:S(2)}) copy-start(bf16[2,512,4,64]{1,0,3,2:T(2,128)(2,1)S(1)} %reshape.466) | copy-start | bytes 1572868
  121.3 24.2 %collective-permute-start.2 = (bf16[1024,512]{1,0:T(8,128)(2,1)}, bf16[1024,512]{1,0:T(8,128)(2,1)}, u32[]{:S(2)}, u32[]{:S(2)}) collective-permute-start(bf16[1024,512]{1,0:T(8,128)(2,1)} %convolution_convert_fusion.6), channel_id=1, source_target_pairs={{1,0},{0,1},{3,2},{2,3},{5,4},{4,5},{7,6},{6,7},{9,8},{8,9},{11,10... | collective-permute-start | bytes 3145736 | tf_op jit(solution)/shard_map/ppermute | solution.py:56
  128.3 49.0 %copy-start.39 = (bf16[2,512,4,64]{1,0,3,2:T(2,128)(2,1)}, bf16[2,512,4,64]{1,0,3,2:T(2,128)(2,1)S(1)}, u32[]{:S(2)}) copy-start(bf16[2,512,4,64]{1,0,3,2:T(2,128)(2,1)S(1)} %reshape.469) | copy-start | bytes 1572868
  130.7 14.8 %copy-start.21 = (bf16[2,512,1024]{2,1,0:T(8,128)(2,1)S(1)}, bf16[2,512,1024]{2,1,0:T(8,128)(2,1)}, u32[]{:S(2)}) copy-start(bf16[2,512,1024]{2,1,0:T(8,128)(2,1)} %get-tuple-element.63) | copy-start | bytes 6291460
  130.8 14.7 %copy-start.54 = (bf16[64,8,2,512]{3,1,2,0:T(8,128)(2,1)S(1)}, bf16[64,8,2,512]{3,1,2,0:T(8,128)(2,1)}, u32[]{:S(2)}) copy-start(bf16[64,8,2,512]{3,1,2,0:T(8,128)(2,1)} %copy-done.53) | copy-start | bytes 3145732
  149.2 56.7 %collective-permute-start.3 = (bf16[1024,512]{1,0:T(8,128)(2,1)S(1)}, bf16[1024,512]{1,0:T(8,128)(2,1)S(1)}, u32[]{:S(2)}, u32[]{:S(2)}) collective-permute-start(bf16[1024,512]{1,0:T(8,128)(2,1)S(1)} %get-tuple-element.84), channel_id=1, source_target_pairs={{1,0},{0,1},{3,2},{2,3},{5,4},{4,5},{7,6},{6,7},{9,8},{8,9},{11,10... | collective-permute-start | bytes 3145736 | tf_op jit(solution)/shard_map/ppermute | solution.py:56
  180.5 25.4 %copy-start.29 = (bf16[2,512,4,2,64]{1,4,3,2,0:T(8,128)(2,1)}, bf16[2,512,4,2,64]{1,4,3,2,0:T(8,128)(2,1)S(1)}, u32[]{:S(2)}) copy-start(bf16[2,512,4,2,64]{1,4,3,2,0:T(8,128)(2,1)S(1)} %fusion.134) | copy-start | bytes 3145732
  181.8 26.1 %copy-start.56 = (bf16[64,8,2,512]{3,1,2,0:T(8,128)(2,1)}, bf16[64,8,2,512]{3,1,2,0:T(8,128)(2,1)S(1)}, u32[]{:S(2)}) copy-start(bf16[64,8,2,512]{3,1,2,0:T(8,128)(2,1)S(1)} %copy.147) | copy-start | bytes 3145732
  182.6 25.3 %collective-permute-start.5 = (bf16[1024,512]{1,0:T(8,128)(2,1)S(1)}, bf16[1024,512]{1,0:T(8,128)(2,1)S(1)}, u32[]{:S(2)}, u32[]{:S(2)}) collective-permute-start(bf16[1024,512]{1,0:T(8,128)(2,1)S(1)} %convolution_convert_fusion.5), channel_id=1, source_target_pairs={{1,0},{0,1},{3,2},{2,3},{5,4},{4,5},{7,6},{6,7},{9,8},{8,9},{11,10... | collective-permute-start | bytes 3145736 | tf_op jit(solution)/shard_map/ppermute | solution.py:56
  184.0 21.9 %collective-permute-start.4 = (f32[1024]{0:T(1024)S(1)}, f32[1024]{0:T(1024)S(1)}, u32[]{:S(2)}, u32[]{:S(2)}) collective-permute-start(f32[1024]{0:T(1024)S(1)} %get-tuple-element.83), channel_id=1, source_target_pairs={{1,0},{0,1},{3,2},{2,3},{5,4},{4,5},{7,6},{6,7},{9,8},{8,9},{11,10... | collective-permute-start | bytes 12296 | tf_op jit(solution)/shard_map/ppermute | solution.py:56
  209.0 21.0 %copy-start.2 = (f32[1024,512]{1,0:T(8,128)}, f32[1024,512]{1,0:T(8,128)S(1)}, u32[]{:S(2)}) copy-start(f32[1024,512]{1,0:T(8,128)S(1)} %convert_add_fusion) | copy-start | bytes 6291460
  219.8 12.7 %copy-start.74 = (bf16[1024,1024]{1,0:T(8,128)(2,1)S(1)}, bf16[1024,1024]{1,0:T(8,128)(2,1)}, u32[]{:S(2)}) copy-start(bf16[1024,1024]{1,0:T(8,128)(2,1)} %multiply_convert_fusion.7) | copy-start | bytes 6291460
  230.3 30.4 %collective-permute-start.8 = (f32[1024]{0:T(1024)S(1)}, f32[1024]{0:T(1024)S(1)}, u32[]{:S(2)}, u32[]{:S(2)}) collective-permute-start(f32[1024]{0:T(1024)S(1)} %get-tuple-element.79), channel_id=1, source_target_pairs={{1,0},{0,1},{3,2},{2,3},{5,4},{4,5},{7,6},{6,7},{9,8},{8,9},{11,10... | collective-permute-start | bytes 12296 | tf_op jit(solution)/shard_map/ppermute | solution.py:56
  231.3 29.5 %collective-permute-start.7 = (bf16[1024,512]{1,0:T(8,128)(2,1)S(1)}, bf16[1024,512]{1,0:T(8,128)(2,1)S(1)}, u32[]{:S(2)}, u32[]{:S(2)}) collective-permute-start(bf16[1024,512]{1,0:T(8,128)(2,1)S(1)} %get-tuple-element.80), channel_id=1, source_target_pairs={{1,0},{0,1},{3,2},{2,3},{5,4},{4,5},{7,6},{6,7},{9,8},{8,9},{11,10... | collective-permute-start | bytes 3145736 | tf_op jit(solution)/shard_map/ppermute | solution.py:56
  259.9 63.5 %collective-permute-start.10 = (bf16[1024,512]{1,0:T(8,128)(2,1)}, bf16[1024,512]{1,0:T(8,128)(2,1)S(1)}, u32[]{:S(2)}, u32[]{:S(2)}) collective-permute-start(bf16[1024,512]{1,0:T(8,128)(2,1)} %fusion.118), channel_id=1, source_target_pairs={{1,0},{0,1},{3,2},{2,3},{5,4},{4,5},{7,6},{6,7},{9,8},{8,9},{11,10... | collective-permute-start | bytes 3145736 | tf_op jit(solution)/shard_map/ppermute | solution.py:56
  261.5 22.9 %slice-start.4 = ((s8[4718592]{0:T(1024)(128)(4,1)}), s8[4194304]{0:T(1024)(128)(4,1)S(1)}, s32[]{:S(2)}) async-start(s8[4718592]{0:T(1024)(128)(4,1)} %bitcast.369), calls=%async_computation.15 | async-start | bytes 8388608
  272.2 12.2 %copy-start.81 = (bf16[1024,1024]{1,0:T(8,128)(2,1)S(1)}, bf16[1024,1024]{1,0:T(8,128)(2,1)}, u32[]{:S(2)}) copy-start(bf16[1024,1024]{1,0:T(8,128)(2,1)} %get-tuple-element.30) | copy-start | bytes 6291460
  272.2 12.2 %copy-start.82 = (bf16[1024,1024]{1,0:T(8,128)(2,1)S(1)}, bf16[1024,1024]{1,0:T(8,128)(2,1)}, u32[]{:S(2)}) copy-start(bf16[1024,1024]{1,0:T(8,128)(2,1)} %get-tuple-element.28) | copy-start | bytes 6291460
  272.2 12.2 %slice-start.5 = ((s8[4718592]{0:T(1024)(128)(4,1)}), s8[524288]{0:T(1024)(128)(4,1)S(1)}, s32[]{:S(2)}) async-start(s8[4718592]{0:T(1024)(128)(4,1)} %bitcast.369), calls=%async_computation.16 | async-start | bytes 1048576
  310.4 12.9 %copy-start.18 = (f32[1024,512]{1,0:T(8,128)S(1)}, f32[1024,512]{1,0:T(8,128)}, u32[]{:S(2)}) copy-start(f32[1024,512]{1,0:T(8,128)} %copy-done.17) | copy-start | bytes 6291460
  310.4 12.9 %copy-start.117 = (f32[1024]{0:T(1024)S(1)}, f32[1024]{0:T(1024)}, u32[]{:S(2)}) copy-start(f32[1024]{0:T(1024)} %copy-done.116) | copy-start | bytes 12292
  310.5 12.9 %copy-start.118 = (f32[512]{0:T(512)S(1)}, f32[512]{0:T(512)}, u32[]{:S(2)}) copy-start(f32[512]{0:T(512)} %dynamic_slice.52) | copy-start | bytes 6148
  322.2 13.6 %copy-start.75 = (bf16[1024,1024]{1,0:T(8,128)(2,1)S(1)}, bf16[1024,1024]{1,0:T(8,128)(2,1)}, u32[]{:S(2)}) copy-start(bf16[1024,1024]{1,0:T(8,128)(2,1)} %multiply_convert_fusion.7) | copy-start | bytes 6291460
  322.2 45.0 %collective-permute-start.15 = (bf16[1024,512]{1,0:T(8,128)(2,1)}, bf16[1024,512]{1,0:T(8,128)(2,1)}, u32[]{:S(2)}, u32[]{:S(2)}) collective-permute-start(bf16[1024,512]{1,0:T(8,128)(2,1)} %fusion.121), channel_id=1, source_target_pairs={{1,0},{0,1},{3,2},{2,3},{5,4},{4,5},{7,6},{6,7},{9,8},{8,9},{11,10... | collective-permute-start | bytes 3145736 | tf_op jit(solution)/shard_map/ppermute | solution.py:56
  334.8 32.3 %collective-permute-start.11 = (f32[1024]{0:T(1024)S(1)}, f32[1024]{0:T(1024)S(1)}, u32[]{:S(2)}, u32[]{:S(2)}) collective-permute-start(f32[1024]{0:T(1024)S(1)} %get-tuple-element.37), channel_id=1, source_target_pairs={{1,0},{0,1},{3,2},{2,3},{5,4},{4,5},{7,6},{6,7},{9,8},{8,9},{11,10... | collective-permute-start | bytes 12296 | tf_op jit(solution)/shard_map/ppermute | solution.py:56
  376.6 25.8 %copy-start.25 = (bf16[2,512,512]{2,1,0:T(8,128)(2,1)S(1)}, bf16[2,512,512]{2,1,0:T(8,128)(2,1)}, u32[]{:S(2)}) copy-start(bf16[2,512,512]{2,1,0:T(8,128)(2,1)} %copy-done.24) | copy-start | bytes 3145732
  381.5 25.6 %collective-permute-start.12 = (bf16[1024,512]{1,0:T(8,128)(2,1)}, bf16[1024,512]{1,0:T(8,128)(2,1)}, u32[]{:S(2)}, u32[]{:S(2)}) collective-permute-start(bf16[1024,512]{1,0:T(8,128)(2,1)} %get-tuple-element.52), channel_id=1, source_target_pairs={{1,0},{0,1},{3,2},{2,3},{5,4},{4,5},{7,6},{6,7},{9,8},{8,9},{11,10... | collective-permute-start | bytes 3145736 | tf_op jit(solution)/shard_map/ppermute | solution.py:56
  382.6 19.8 %collective-permute-start.16 = (f32[1024]{0:T(1024)S(1)}, f32[1024]{0:T(1024)S(1)}, u32[]{:S(2)}, u32[]{:S(2)}) collective-permute-start(f32[1024]{0:T(1024)S(1)} %get-tuple-element.120), channel_id=1, source_target_pairs={{1,0},{0,1},{3,2},{2,3},{5,4},{4,5},{7,6},{6,7},{9,8},{8,9},{11,10... | collective-permute-start | bytes 12296 | tf_op jit(solution)/shard_map/ppermute | solution.py:56
  405.6 44.3 %collective-permute-start.17 = (bf16[1024,512]{1,0:T(8,128)(2,1)}, bf16[1024,512]{1,0:T(8,128)(2,1)}, u32[]{:S(2)}, u32[]{:S(2)}) collective-permute-start(bf16[1024,512]{1,0:T(8,128)(2,1)} %fusion.218), channel_id=1, source_target_pairs={{1,0},{0,1},{3,2},{2,3},{5,4},{4,5},{7,6},{6,7},{9,8},{8,9},{11,10... | collective-permute-start | bytes 3145736 | tf_op jit(solution)/shard_map/ppermute | solution.py:56
  500.2 165.3 %reduce-scatter.5.cloned.1.call-start = ((), (), s32[]{:S(2)}) async-start(), calls=%async_computation.7 | async-start | bytes 2228224 | tf_op jit(solution)/shard_map/reduce_scatter | solution.py:47
  515.9 185.0 %reduce-scatter.11.cloned.1.call-start = ((), (), s32[]{:S(2)}) async-start(), calls=%async_computation.10 | async-start | bytes 5013504 | tf_op jit(solution)/shard_map/reduce_scatter | solution.py:47
  516.5 299.4 %reduce-scatter.9.cloned.1.call-start = ((), (), s32[]{:S(2)}) async-start(), calls=%async_computation.9 | async-start | bytes 10027008 | tf_op jit(solution)/shard_map/reduce_scatter | solution.py:47
  524.0 26.4 %collective-permute-start.6 = (bf16[1024,512]{1,0:T(8,128)(2,1)}, bf16[1024,512]{1,0:T(8,128)(2,1)}, u32[]{:S(2)}, u32[]{:S(2)}) collective-permute-start(bf16[1024,512]{1,0:T(8,128)(2,1)} %fusion.124), channel_id=1, source_target_pairs={{1,0},{0,1},{3,2},{2,3},{5,4},{4,5},{7,6},{6,7},{9,8},{8,9},{11,10... | collective-permute-start | bytes 3145736 | tf_op jit(solution)/shard_map/ppermute | solution.py:56
  526.4 32.9 %copy-start.76 = (bf16[1024,1024]{1,0:T(8,128)(2,1)}, bf16[1024,1024]{1,0:T(8,128)(2,1)S(1)}, u32[]{:S(2)}) copy-start(bf16[1024,1024]{1,0:T(8,128)(2,1)S(1)} %slice.147) | copy-start | bytes 6291460
  526.5 23.9 %copy-start.20 = (f32[1024,512]{1,0:T(8,128)S(1)}, f32[1024,512]{1,0:T(8,128)}, u32[]{:S(2)}) copy-start(f32[1024,512]{1,0:T(8,128)} %copy-done.17) | copy-start | bytes 6291460
  533.0 23.3 %copy-start.102 = (bf16[1024,512]{0,1:T(8,128)(2,1)S(1)}, bf16[1024,512]{0,1:T(8,128)(2,1)}, u32[]{:S(2)}) copy-start(bf16[1024,512]{0,1:T(8,128)(2,1)} %copy-done.101) | copy-start | bytes 3145732
  533.0 39.7 %collective-permute-start.9 = (bf16[1024,512]{1,0:T(8,128)(2,1)S(1)}, bf16[1024,512]{1,0:T(8,128)(2,1)S(1)}, u32[]{:S(2)}, u32[]{:S(2)}) collective-permute-start(bf16[1024,512]{1,0:T(8,128)(2,1)S(1)} %fusion.127), channel_id=1, source_target_pairs={{1,0},{0,1},{3,2},{2,3},{5,4},{4,5},{7,6},{6,7},{9,8},{8,9},{11,10... | collective-permute-start | bytes 3145736 | tf_op jit(solution)/shard_map/ppermute | solution.py:56
  556.4 16.4 %slice-start.2 = ((s8[4718592]{0:T(1024)(128)(4,1)}), s8[4194304]{0:T(1024)(128)(4,1)S(1)}, s32[]{:S(2)}) async-start(s8[4718592]{0:T(1024)(128)(4,1)} %bitcast.367), calls=%async_computation.13 | async-start | bytes 8388608
  556.4 16.4 %slice-start.6 = ((s8[4718592]{0:T(1024)(128)(4,1)}), s8[4194304]{0:T(1024)(128)(4,1)S(1)}, s32[]{:S(2)}) async-start(s8[4718592]{0:T(1024)(128)(4,1)} %bitcast.371), calls=%async_computation.17 | async-start | bytes 8388608
  558.7 14.1 %slice-start.3 = ((s8[4718592]{0:T(1024)(128)(4,1)}), s8[524288]{0:T(1024)(128)(4,1)S(1)}, s32[]{:S(2)}) async-start(s8[4718592]{0:T(1024)(128)(4,1)} %bitcast.367), calls=%async_computation.14 | async-start | bytes 1048576
  558.7 14.1 %slice-start.7 = ((s8[4718592]{0:T(1024)(128)(4,1)}), s8[524288]{0:T(1024)(128)(4,1)S(1)}, s32[]{:S(2)}) async-start(s8[4718592]{0:T(1024)(128)(4,1)} %bitcast.371), calls=%async_computation.18 | async-start | bytes 1048576
  558.7 36.7 %collective-permute-start.13 = (bf16[1024,512]{1,0:T(8,128)(2,1)}, bf16[1024,512]{1,0:T(8,128)(2,1)}, u32[]{:S(2)}, u32[]{:S(2)}) collective-permute-start(bf16[1024,512]{1,0:T(8,128)(2,1)} %convolution_convert_fusion.2), channel_id=1, source_target_pairs={{1,0},{0,1},{3,2},{2,3},{5,4},{4,5},{7,6},{6,7},{9,8},{8,9},{11,10... | collective-permute-start | bytes 3145736 | tf_op jit(solution)/shard_map/ppermute | solution.py:56
  561.6 49.6 %collective-permute-start.18 = (bf16[1024,512]{1,0:T(8,128)(2,1)}, bf16[1024,512]{1,0:T(8,128)(2,1)}, u32[]{:S(2)}, u32[]{:S(2)}) collective-permute-start(bf16[1024,512]{1,0:T(8,128)(2,1)} %convolution_convert_fusion), channel_id=1, source_target_pairs={{1,0},{0,1},{3,2},{2,3},{5,4},{4,5},{7,6},{6,7},{9,8},{8,9},{11,10... | collective-permute-start | bytes 3145736 | tf_op jit(solution)/shard_map/ppermute | solution.py:56
  575.5 19.8 %copy-start.115 = (f32[1,4,2,128]{3,1,2,0:T(4,128)S(1)}, f32[1,4,2,128]{3,1,2,0:T(4,128)}, u32[]{:S(2)}) copy-start(f32[1,4,2,128]{3,1,2,0:T(4,128)} %copy-done.114) | copy-start | bytes 12292
  577.2 34.0 %copy-start.77 = (bf16[1024,1024]{1,0:T(8,128)(2,1)S(1)}, bf16[1024,1024]{1,0:T(8,128)(2,1)}, u32[]{:S(2)}) copy-start(bf16[1024,1024]{1,0:T(8,128)(2,1)} %copy-done.76) | copy-start | bytes 6291460
  577.3 34.0 %copy-start.97 = (bf16[1024,4,128]{0,2,1:T(8,128)(2,1)S(1)}, bf16[1024,4,128]{0,2,1:T(8,128)(2,1)}, u32[]{:S(2)}) copy-start(bf16[1024,4,128]{0,2,1:T(8,128)(2,1)} %copy-done.95) | copy-start | bytes 3145732
  577.3 34.0 %copy-start.100 = (bf16[1024,512]{0,1:T(8,128)(2,1)S(1)}, bf16[1024,512]{0,1:T(8,128)(2,1)}, u32[]{:S(2)}) copy-start(bf16[1024,512]{0,1:T(8,128)(2,1)} %copy-done.98) | copy-start | bytes 3145732
  599.4 14.7 %copy-start.11 = (bf16[2,512,1024]{2,1,0:T(8,128)(2,1)S(1)}, bf16[2,512,1024]{2,1,0:T(8,128)(2,1)}, u32[]{:S(2)}) copy-start(bf16[2,512,1024]{2,1,0:T(8,128)(2,1)} %copy-done.9) | copy-start | bytes 6291460
  599.4 14.7 %copy-start.22 = (bf16[2,512,1024]{2,1,0:T(8,128)(2,1)S(1)}, bf16[2,512,1024]{2,1,0:T(8,128)(2,1)}, u32[]{:S(2)}) copy-start(bf16[2,512,1024]{2,1,0:T(8,128)(2,1)} %get-tuple-element.63) | copy-start | bytes 6291460
  599.4 14.7 %copy-start.31 = (f32[1024,512]{1,0:T(8,128)S(1)}, f32[1024,512]{1,0:T(8,128)}, u32[]{:S(2)}) copy-start(f32[1024,512]{1,0:T(8,128)} %get-tuple-element.53) | copy-start | bytes 6291460
  599.4 14.7 %copy-start.113 = (f32[1,4,2,128]{3,1,2,0:T(4,128)S(1)}, f32[1,4,2,128]{3,1,2,0:T(4,128)}, u32[]{:S(2)}) copy-start(f32[1,4,2,128]{3,1,2,0:T(4,128)} %copy-done.112) | copy-start | bytes 12292
  599.5 14.6 %collective-permute-start.14 = (f32[1024]{0:T(1024)S(1)}, f32[1024]{0:T(1024)S(1)}, u32[]{:S(2)}, u32[]{:S(2)}) collective-permute-start(f32[1024]{0:T(1024)S(1)} %get-tuple-element.43), channel_id=1, source_target_pairs={{1,0},{0,1},{3,2},{2,3},{5,4},{4,5},{7,6},{6,7},{9,8},{8,9},{11,10... | collective-permute-start | bytes 12296 | tf_op jit(solution)/shard_map/ppermute | solution.py:56
  614.2 44.1 %copy-start.26 = (bf16[2,512,512]{2,1,0:T(8,128)(2,1)S(1)}, bf16[2,512,512]{2,1,0:T(8,128)(2,1)}, u32[]{:S(2)}) copy-start(bf16[2,512,512]{2,1,0:T(8,128)(2,1)} %copy-done.24) | copy-start | bytes 3145732
  616.6 41.7 %collective-permute-start.19 = (f32[1024]{0:T(1024)S(1)}, f32[1024]{0:T(1024)S(1)}, u32[]{:S(2)}, u32[]{:S(2)}) collective-permute-start(f32[1024]{0:T(1024)S(1)} %get-tuple-element.41), channel_id=1, source_target_pairs={{1,0},{0,1},{3,2},{2,3},{5,4},{4,5},{7,6},{6,7},{9,8},{8,9},{11,10... | collective-permute-start | bytes 12296 | tf_op jit(solution)/shard_map/ppermute | solution.py:56
  (107 other events, 512.0 us)
Sparse Core Ops, SparseCore 0:
  10.9 48.1 all-gather.3
  61.3 52.1 all-gather.7
  116.4 79.9 all-gather.5
  500.3 57.3 reduce-scatter.6
  561.7 60.5 reduce-scatter.4
  626.1 74.7 reduce-scatter.10
  705.5 110.3 reduce-scatter.8

commit v2 on v1

--- a/solution.py
+++ b/solution.py
@@ -75,6 +75,17 @@
     for step in range(1, parts):
         total = total + shift(value, step)
     return total
+
+
+def total_of(value, axis):
+    count = lax.axis_size(axis)
+    if count & (count - 1):
+        return lax.psum(value, axis)
+    bit = 1
+    while bit < count:
+        value = value + lax.ppermute(value, axis, [(i, i ^ bit) for i in range(count)])
+        bit *= 2
+    return value
 
 
 def branch(value, rows):
@@ -247,7 +258,7 @@
 
     down_total = over_tokens(grad_whole, hidden)
     grad_whole[-1], down_total = after(grad_whole[-1], down_total)
-    down_sum = scatter_rows(down_total).T
+    down_sum = scatter_rows(down_total)
     grad_gateup, grad_second = [], []
     for i in run:
         gate, upper, sigmoid_gate = gates[i]
@@ -259,8 +270,9 @@
         )
         grad_second.append(branch(grad_gateup[i], gateup_rows))
     gateup_total = over_tokens(normed_second, grad_gateup)
-    grad_second[-1], gateup_total = after(grad_second[-1], gateup_total)
-    gateup_sum = scatter_rows(gateup_total).reshape(rows, 2, ff)
+    grad_second[-1], gateup_total, *mixed = after(grad_second[-1], gateup_total, *mixed)
+    gateup_total, down_sum = after(gateup_total, down_sum)
+    gateup_sum = scatter_rows(gateup_total)
 
     def slice_norm_back(grad, unit, scale, gain):
         scaled = grad * gain
@@ -277,7 +289,6 @@
         grad_branch.append(whole(grad_resid[i].astype(bf16)))
     out_total = over_tokens(grad_branch, attended)
     grad_branch[-1], out_total = after(grad_branch[-1], out_total)
-    out_sum = scatter_rows(out_total).T
 
     grad_qkv, grad_input = [], []
     first_gain = pair_gain = 0.0
@@ -311,12 +322,15 @@
         first_gain = first_gain + gain
         pair_gain = pair_gain + jnp.stack([query_gain_grad, key_gain_grad])
         grad_input.append(back + grad_resid[i])
-    qkv_sum = scatter_rows(over_tokens(normed_first, grad_qkv))
+    attn_total = jnp.concatenate([over_tokens(normed_first, grad_qkv), out_total], axis=1)
+    attn_total, gateup_sum = after(attn_total, gateup_sum)
+    attn_sum = scatter_rows(attn_total)
+    qkv_sum, out_sum = attn_sum[:, : cols + kv_cols], attn_sum[:, cols + kv_cols :].T
 
     gains = jnp.zeros((2 * model,), f32)
     gains = lax.dynamic_update_slice_in_dim(gains, first_gain, offset, 0)
     gains = lax.dynamic_update_slice_in_dim(gains, second_gain, model + offset, 0)
-    gains = lax.psum(jnp.concatenate([gains, pair_gain.reshape(-1)]), ("dp", "mp"))
+    gains = total_of(total_of(jnp.concatenate([gains, pair_gain.reshape(-1)]), "mp"), "dp")
 
     def joined(pieces):
         return jnp.concatenate(pieces, axis=0).reshape(sequences, length, width)
@@ -330,8 +344,8 @@
         out_sum,
         gains[2 * model :].reshape(2, HEAD_SIZE),
         gains[model : 2 * model],
-        gateup_sum,
-        down_sum,
+        gateup_sum.reshape(rows, 2, ff),
+        down_sum.T,
     )
 
 

time: 830 us -> 669 us (0.81)
  waiting for transfers between devices: 276 us -> 142 us
  blocking collectives: 39.8 us -> 0 us
  other arithmetic: 110 us -> 100 us
  local copies, waits for them, and re-layouts: 88.1 us -> 98 us
    reduce_scatter x4 -> x2, waiting for transfers between devices: 146 us -> 0.01 us  [scatter_rows(): lax.psum_scatter(total, 'dp', scatter_dimension=0, tiled=True).astype(f32)]
    psum x1 -> x0, blocking collectives: 39.8 us -> none  [body(): lax.psum(jnp.concatenate([gains, pair_gain.reshape(-1)]), ('dp', 'mp'))]
    unnamed x7, waiting for transfers between devices: 1.77 us -> 21.1 us
    ppermute x20, waiting for transfers between devices: 128 us -> 115 us  [shift(): lax.ppermute(value, 'mp', [((i + step) % parts, i) for i in range(parts)])]
    unnamed x298 -> x283, local copies, waits for them, and re-layouts: 24.1 us -> 32.7 us
  transfers between devices with their start and end apart: 27 -> 31, of which waited for: 11 -> 14; matrix products, arithmetic and copies ran while one was open for 45% -> 62% of each run, Pallas kernels for 0% -> 0%
where the time goes in v2:
time: 669 us; the launch traced here: 664 us
  matrix products  279 us (42%)
  waiting for transfers between devices  142 us (21%)
  other arithmetic  100 us (15%)
  local copies, waits for them, and re-layouts  98 us (15%)
  starting transfers between devices  28.1 us (4%)
  between operations  16.5 us (2%)
    ppermute x20, waiting for transfers between devices, shift(): lax.ppermute(value, 'mp', [((i + step) % parts, i) for i in range(parts)])  115 us
    dot_general x16, matrix products, term(): lax.dot_general(value, piece, (((1,), (1,)), ((), ())), preferred_element...  81.6 us
    dot_general x4, matrix products, over_tokens(): lax.dot_general(left, right, (((0,), (0,)), ((), ())), preferred_element_...  52.4 us
    unnamed x283, local copies, waits for them, and re-layouts  32.7 us
    dot_general x2, matrix products, body(): jnp.dot(normed_second[i], gateup_rows[:, ff:], preferred_element_type=f32)  30.7 us
    dot_general x2, matrix products, body(): grad_hidden = jnp.dot(grad_whole[i], down_rows, preferred_element_type=f32)  25.1 us
    ppermute x20, starting transfers between devices, shift(): lax.ppermute(value, 'mp', [((i + step) % parts, i) for i in range(parts)])  22.5 us
    unnamed x7, waiting for transfers between devices  21.1 us
  transfers between devices with their start and end apart: 31, of which 14 were waited for; matrix products, arithmetic and copies ran while one was open for 62% of the time, Pallas kernels for 0%

profile of v2, /device:TPU:0, one launch (start us, length us, event | category | flops | bytes accessed | tf_op | source)
XLA Modules:
  0.0 663.8 jit_solution(5370415939230487613)
XLA Ops:
  10.5 2.7 fusion.222
  13.3 2.9 collective-permute-start.1
  17.3 3.3 multiply_reduce_fusion
  26.0 2.5 fusion.171
  28.5 4.1 multiply_convert_fusion.8
  32.6 7.7 %collective-permute-done.1 = bf16[1024,512]{1,0:T(8,128)(2,1)} collective-permute-done((bf16[1024,512]{1,0:T(8,128)(2,1)S(1)}, bf16[1024,512]{1,0:T(8,128)(2,1)}, u32[]{:S(2)}, u32[]{:S(2)}) %collective-permute-start.1) | collective-permute-done | bytes 1048608 | tf_op jit(solution)/shard_map/ppermute | solution.py:56
  41.7 20.3 %collective-permute-done = bf16[1024,512]{1,0:T(8,128)(2,1)} collective-permute-done((bf16[1024,512]{1,0:T(8,128)(2,1)}, bf16[1024,512]{1,0:T(8,128)(2,1)}, u32[]{:S(2)}, u32[]{:S(2)}) %collective-permute-start) | collective-permute-done | bytes 1048608 | tf_op jit(solution)/shard_map/ppermute | solution.py:56
  63.6 2.7 pad_maximum_fusion.8
  68.6 4.0 fusion.215
  75.4 5.1 fusion.217
  107.2 11.0 %fusion.226 = (f32[2,4,2,512]{3,2,1,0:T(2,128)S(1)}, f32[2,4,2,512,512]{3,4,2,1,0:T(8,128)}) fusion(pred[2,512,512]{1,2,0:T(8,128)(4,1)} %get-tuple-element.155, bf16[2,512,4,2,64]{1,4,3,2,0:T(8,128)(2,1)S(1)} %copy_dynamic-update-slice_fusion, bf16[2,512,4,32]{1,3,2,0:T(8,128)(2,1)} %bitcast.335, bf16[2,512,4,32]{1,3,2,0:T(8,128)(2,1)S(1)} %bitcast.333), kind=kOutput, calls=%fused_computation.363 | convolution fusion | flops 554697216 | bytes 18907136 | tf_op jit(solution)/shard_map/vmap()/sub | solution.py:133
  118.2 7.6 %divide_convert_fusion.1 = bf16[2,4,2,512,512]{3,4,2,1,0:T(8,128)(2,1)S(1)} fusion(f32[2,4,2,512,512]{3,4,2,1,0:T(8,128)} %get-tuple-element.185, f32[2,4,2,512]{3,2,1,0:T(2,128)S(1)} %get-tuple-element.184), kind=kLoop, calls=%fused_computation.20 | loop fusion | flops 8388608 | bytes 25198592 | tf_op jit(solution)/shard_map/vmap()/convert_element_type | solution.py:135
  133.4 8.4 %bitcast_select_fusion.1 = f32[2,4,2,512,512]{3,4,2,1,0:T(8,128)} fusion(pred[2,512,512]{1,2,0:T(8,128)(4,1)S(1)} %copy-done.36, bf16[2,512,4,2,64]{1,4,3,2,0:T(8,128)(2,1)S(1)} %copy_dynamic-update-slice_fusion.2, bf16[2,512,4,32]{1,3,2,0:T(8,128)(2,1)S(1)} %bitcast.327, bf16[2,512,4,32]{1,3,2,0:T(8,128)(2,1)S(1)} %bitcast.325), kind=kOutput, calls=%fused_computation.17 | convolution fusion | flops 546308096 | bytes 18874368 | tf_op jit(solution)/shard_map/vmap(qhgd,khd->hgqk)/dot_general | solution.py:124
  141.9 13.9 %collective-permute-done.2 = bf16[1024,512]{1,0:T(8,128)(2,1)S(1)} collective-permute-done((bf16[1024,512]{1,0:T(8,128)(2,1)S(1)}, bf16[1024,512]{1,0:T(8,128)(2,1)S(1)}, u32[]{:S(2)}, u32[]{:S(2)}) %collective-permute-start.2) | collective-permute-done | bytes 1048608 | tf_op jit(solution)/shard_map/ppermute | solution.py:56
  159.8 19.0 %fusion.227 = (f32[2,4,2,512]{3,2,1,0:T(2,128)S(1)}, f32[2,4,2,512,512]{3,4,2,1,0:T(8,128)}) fusion(f32[2,4,2,512,512]{3,4,2,1,0:T(8,128)} %bitcast_select_fusion.1), kind=kOutput, calls=%fused_computation.364 | output fusion | flops 8389119 | bytes 33587200 | tf_op jit(solution)/shard_map/vmap()/sub | solution.py:133
  178.9 7.4 %divide_convert_fusion = bf16[2,4,2,512,512]{3,4,2,1,0:T(8,128)(2,1)S(1)} fusion(f32[2,4,2,512,512]{3,4,2,1,0:T(8,128)} %get-tuple-element.187, f32[2,4,2,512]{3,2,1,0:T(2,128)S(1)} %get-tuple-element.186), kind=kLoop, calls=%fused_computation.18 | loop fusion | flops 8388608 | bytes 25198592 | tf_op jit(solution)/shard_map/vmap()/convert_element_type | solution.py:135
  193.9 21.0 %collective-permute-done.4 = f32[1024]{0:T(1024)S(1)} collective-permute-done((f32[1024]{0:T(1024)S(1)}, f32[1024]{0:T(1024)S(1)}, u32[]{:S(2)}, u32[]{:S(2)}) %collective-permute-start.4) | collective-permute-done | bytes 4128 | tf_op jit(solution)/shard_map/ppermute | solution.py:56
  217.7 10.7 %fusion.228 = f32[1024,2304]{1,0:T(8,128)} fusion(bf16[1024,1024]{1,0:T(8,128)(2,1)} %get-tuple-element.30, bf16[1024,2304]{1,0:T(8,128)(2,1)} %all-gather.8.cloned.1.call-done), kind=kOutput, calls=%fused_computation.365 | convolution fusion | flops 4831838208 | bytes 16252928 | tf_op jit(solution)/shard_map/dot_general | solution.py:265
  228.4 10.3 %fusion.63 = f32[1024,2304]{1,0:T(8,128)} fusion(bf16[1024,1024]{1,0:T(8,128)(2,1)} %multiply_convert_fusion.7, bf16[1024,4608]{1,0:T(8,128)(2,1)} %all-gather.6.cloned.1.call-done), kind=kOutput, calls=%fused_computation.84 | convolution fusion | flops 4831838208 | bytes 16252928 | tf_op jit(solution)/shard_map/dot_general | solution.py:249
  238.7 18.0 %multiply_convert_fusion.1 = (bf16[1024,2304]{1,0:T(8,128)(2,1)}, bf16[1024,2304]{1,0:T(8,128)(2,1)}, bf16[1024,2304]{1,0:T(8,128)(2,1)}) fusion(f32[1024,2304]{1,0:T(8,128)} %fusion.63, f32[1024,2304]{1,0:T(8,128)} %fusion.228, bf16[1024,1024]{1,0:T(8,128)(2,1)S(1)} %copy-done.68, bf16[1024,4608]{1,0:T(8,128)(2,1)} %all-gather.6.cloned.1.call-done), kind=kOutput, calls=%fused_computation.31 | convolution fusion | flops 4869586944 | bytes 39845888 | tf_op jit(solution)/shard_map/dot_general | solution.py:252
  256.7 9.2 %fusion.121 = bf16[1024,512]{1,0:T(8,128)(2,1)S(1)} fusion(bf16[1024,4608]{1,0:T(8,128)(2,1)} %all-gather.6.cloned.1.call-done, s32[]{:T(128)S(6)} %select_n.97, bf16[1024,2304]{1,0:T(8,128)(2,1)} %get-tuple-element.108, bf16[1024,2304]{1,0:T(8,128)(2,1)} %get-tuple-element.106), kind=kOutput, calls=%fused_computation.180 | convolution fusion | flops 4851236864 | bytes 15204356 | tf_op jit(solution)/shard_map/dot_general | solution.py:98
  268.8 5.4 fusion.124
  275.8 16.3 %collective-permute-done.7 = f32[1024]{0:T(1024)S(1)} collective-permute-done((f32[1024]{0:T(1024)S(1)}, f32[1024]{0:T(1024)S(1)}, u32[]{:S(2)}, u32[]{:S(2)}) %collective-permute-start.7) | collective-permute-done | bytes 4128 | tf_op jit(solution)/shard_map/ppermute | solution.py:56
  292.2 12.2 %multiply_reduce_fusion.3 = (f32[512]{0:T(512)}, f32[1024]{0:T(1024)S(1)}, f32[1024,512]{1,0:T(8,128)}) fusion(f32[1024,512]{1,0:T(8,128)S(1)} %copy-done.23, f32[1024]{0:T(1024)S(1)} %add_rsqrt_fusion.5, bf16[1024,512]{1,0:T(8,128)(2,1)S(1)} %collective-permute-done.11, f32[512]{0:T(512)S(1)} %dynamic_slice.52, ...), kind=kOutput, calls=%fused_computation.143 | convolution fusion | flops 4854905344 | bytes 19410948 | tf_op jit(solution)/shard_map/dot_general | solution.py:98
  304.5 10.2 %collective-permute-done.6 = bf16[1024,512]{1,0:T(8,128)(2,1)S(1)} collective-permute-done((bf16[1024,512]{1,0:T(8,128)(2,1)S(1)}, bf16[1024,512]{1,0:T(8,128)(2,1)S(1)}, u32[]{:S(2)}, u32[]{:S(2)}) %collective-permute-start.6) | collective-permute-done | bytes 1048608 | tf_op jit(solution)/shard_map/ppermute | solution.py:56
  315.4 7.4 %fusion.61 = f32[1024,2304]{1,0:T(8,128)} fusion(bf16[1024,1024]{1,0:T(8,128)(2,1)S(1)} %multiply_convert_fusion.6, bf16[1024,4608]{1,0:T(8,128)(2,1)S(1)} %bitcast.369), kind=kOutput, calls=%fused_computation.82 | convolution fusion | flops 4831838208 | bytes 16252928 | tf_op jit(solution)/shard_map/dot_general | solution.py:249
  322.8 12.7 %multiply_convert_fusion.4 = (bf16[1024,2304]{1,0:T(8,128)(2,1)}, f32[1024,2304]{1,0:T(8,128)}) fusion(f32[1024,2304]{1,0:T(8,128)} %fusion.61, bf16[1024,1024]{1,0:T(8,128)(2,1)S(1)} %multiply_convert_fusion.6, bf16[1024,4608]{1,0:T(8,128)(2,1)} %all-gather.6.cloned.1.call-done), kind=kOutput, calls=%fused_computation.34 | convolution fusion | flops 4845993984 | bytes 30408704 | tf_op jit(solution)/shard_map/dot_general | solution.py:252
  335.5 13.3 %fusion.29 = bf16[1024,2304]{1,0:T(8,128)(2,1)} fusion(bf16[1024,2304]{1,0:T(8,128)(2,1)} %get-tuple-element.188, bf16[1024,2304]{1,0:T(8,128)(2,1)S(1)} %bitcast.373, bf16[1024,1024]{1,0:T(8,128)(2,1)S(1)} %copy-done.73, bf16[1024,1024]{1,0:T(8,128)(2,1)S(1)} %copy-done.75), kind=kOutput, calls=%fused_computation.45 | convolution fusion | flops 9693298688 | bytes 18350080 | tf_op jit(solution)/shard_map/dot_general | solution.py:114
  348.9 6.8 %fusion.127 = bf16[1024,512]{1,0:T(8,128)(2,1)} fusion(bf16[1024,2304]{1,0:T(8,128)(2,1)} %get-tuple-element.188, bf16[1024,2304]{1,0:T(8,128)(2,1)} %all-gather.8.cloned.1.call-done, s32[]{:T(128)S(6)} %select_n.97), kind=kOutput, calls=%fused_computation.182 | convolution fusion | flops 2416443392 | bytes 8126468 | tf_op jit(solution)/shard_map/dot_general | solution.py:98
  356.1 14.4 %multiply_convert_fusion.3 = (bf16[1024,2304]{1,0:T(8,128)(2,1)}, bf16[1024,2304]{1,0:T(8,128)(2,1)}) fusion(f32[1024,2304]{1,0:T(8,128)S(1)} %copy-done.125, f32[1024,2304]{1,0:T(8,128)} %get-tuple-element.189, bf16[1024,1024]{1,0:T(8,128)(2,1)S(1)} %copy-done.74, bf16[1024,2304]{1,0:T(8,128)(2,1)} %all-gather.8.cloned.1.call-done), kind=kOutput, calls=%fused_computation.33 | convolution fusion | flops 4862509056 | bytes 35127296 | tf_op jit(solution)/shard_map/dot_general | solution.py:265
  370.5 31.2 %fusion.15 = bf16[1024,4608]{1,0:T(8,128)(2,1)} fusion(bf16[1024,2304]{1,0:T(8,128)(2,1)} %get-tuple-element.110, bf16[1024,2304]{1,0:T(8,128)(2,1)} %get-tuple-element.109, bf16[1024,2304]{1,0:T(8,128)(2,1)} %get-tuple-element.108, bf16[1024,2304]{1,0:T(8,128)(2,1)} %get-tuple-element.106, bf16[1024,1024]{1,0:T(8,128)(2,1)} %copy-done.70, ...), kind=kOutput, calls=%fused_computation.23 | convolution fusion | flops 19415957504 | bytes 32505856 | tf_op jit(solution)/shard_map/dot_general | solution.py:114
  401.7 9.5 %fusion.118 = bf16[1024,512]{1,0:T(8,128)(2,1)S(1)} fusion(bf16[1024,4608]{1,0:T(8,128)(2,1)} %all-gather.6.cloned.1.call-done, s32[]{:T(128)S(6)} %select_n.97, bf16[1024,2304]{1,0:T(8,128)(2,1)} %get-tuple-element.110, bf16[1024,2304]{1,0:T(8,128)(2,1)} %get-tuple-element.109), kind=kOutput, calls=%fused_computation.179 | convolution fusion | flops 4851236864 | bytes 15204356 | tf_op jit(solution)/shard_map/dot_general | solution.py:98
  412.9 6.8 %add_convert_fusion.1 = bf16[1024,512]{1,0:T(8,128)(2,1)} fusion(f32[1024,512]{1,0:T(8,128)S(1)} %copy-done.24, bf16[1024,512]{1,0:T(8,128)(2,1)S(1)} %collective-permute-done.9, bf16[1024,2304]{1,0:T(8,128)(2,1)} %get-tuple-element.107, bf16[1024,2304]{1,0:T(8,128)(2,1)} %all-gather.8.cloned.1.call-done, s32[]{:T(128)S(6)} %select_n.95), kind=kOutput, calls=%fused_computation.158 | convolution fusion | flops 2418016256 | bytes 11272196 | tf_op jit(solution)/shard_map/dot_general | solution.py:98
  419.8 7.1 %add_convert_fusion = bf16[1024,512]{1,0:T(8,128)(2,1)} fusion(f32[1024,512]{1,0:T(8,128)S(1)} %copy-done.4, bf16[1024,512]{1,0:T(8,128)(2,1)} %collective-permute-done.10, bf16[1024,2304]{1,0:T(8,128)(2,1)} %get-tuple-element.188, bf16[1024,2304]{1,0:T(8,128)(2,1)} %all-gather.8.cloned.1.call-done, s32[]{:T(128)S(6)} %select_n.95), kind=kOutput, calls=%fused_computation.157 | convolution fusion | flops 2418016256 | bytes 11272196 | tf_op jit(solution)/shard_map/dot_general | solution.py:98
  428.2 7.8 %convert_add_fusion.7 = f32[1024,512]{1,0:T(8,128)S(1)} fusion(bf16[1024,512]{1,0:T(8,128)(2,1)} %collective-permute-done.8, bf16[1024,4608]{1,0:T(8,128)(2,1)S(1)} %bitcast.371, s32[]{:T(128)S(6)} %select_n.95, bf16[1024,2304]{1,0:T(8,128)(2,1)} %get-tuple-element.110, bf16[1024,2304]{1,0:T(8,128)(2,1)} %get-tuple-element.109), kind=kOutput, calls=%fused_computation.159 | convolution fusion | flops 4851761152 | bytes 17301508 | tf_op jit(solution)/shard_map/dot_general | solution.py:98
  436.0 4.2 fusion.220
  444.5 3.3 slice.155
  447.8 14.1 %collective-permute-done.16 = f32[1024]{0:T(1024)S(1)} collective-permute-done((f32[1024]{0:T(1024)S(1)}, f32[1024]{0:T(1024)S(1)}, u32[]{:S(2)}, u32[]{:S(2)}) %collective-permute-start.16) | collective-permute-done | bytes 4128 | tf_op jit(solution)/shard_map/ppermute | solution.py:56
  468.4 2.5 fusion.130
  470.8 2.5 reshape.489
  473.4 4.7 copy.130
  479.6 6.9 %fusion.148 = bf16[2,4,8,8,512]{4,3,2,1,0:T(8,128)(2,1)} fusion(bf16[2,512,4,2,64]{1,4,3,2,0:T(8,128)(2,1)S(1)} %copy.130, bf16[2,4,2,512,512]{3,4,2,1,0:T(8,128)(2,1)} %copy-done.1), kind=kOutput, calls=%fused_computation.206 | convolution fusion | flops 537133056 | bytes 9961472 | tf_op jit(solution)/shard_map/vmap(hgqk,qhgd->khd)/dot_general | solution.py:149
  486.5 4.9 fusion.13
  491.5 2.6 fusion.138
  495.6 3.0 copy.133
  498.7 4.3 reshape.466
  510.5 3.4 fusion.113
  513.8 2.5 convolution_convert_fusion.1
  518.4 4.6 copy.141
  524.6 5.3 fusion.11
  533.3 2.9 copy.144
  536.2 4.2 reshape.469
  540.5 6.4 fusion.136
  548.0 6.1 fusion.147
  560.1 3.4 multiply_reduce_fusion.7
  573.1 4.5 fusion.108
  580.7 4.9 copy.180
  585.7 4.1 convolution_convert_fusion
  591.8 4.7 fusion.79
  597.0 10.5 %collective-permute-done.18 = bf16[1024,512]{1,0:T(8,128)(2,1)} collective-permute-done((bf16[1024,512]{1,0:T(8,128)(2,1)}, bf16[1024,512]{1,0:T(8,128)(2,1)}, u32[]{:S(2)}, u32[]{:S(2)}) %collective-permute-start.18) | collective-permute-done | bytes 1048608 | tf_op jit(solution)/shard_map/ppermute | solution.py:56
  607.5 2.5 convert_add_fusion.2
  618.6 2.5 collective-permute-done.22
  626.9 2.5 pad_maximum_fusion.6
  632.6 20.3 %reduce-scatter.10.cloned.1.call-done = bf16[64,1536]{1,0:T(8,128)(2,1)} async-done(((bf16[1024,1536]{1,0:T(8,128)(2,1)}), bf16[64,1536]{1,0:T(8,128)(2,1)}) %reduce-scatter.10.cloned.1.call-update) | async-done | bytes 196624
  (468 shorter events, 146.1 us)
Async XLA Ops:
  7.2 59.1 %all-gather.4.cloned.1.call-start = ((), (), s32[]{:S(2)}) async-start(), calls=%async_computation.3 | async-start | bytes 3342336 | tf_op jit(solution)/shard_map/all_gather | solution.py:43
  9.7 208.0 %all-gather.8.cloned.1.call-start = ((), (), s32[]{:S(2)}) async-start(), calls=%async_computation.5 | async-start | bytes 5013504 | tf_op jit(solution)/shard_map/all_gather | solution.py:43
  10.5 217.9 %all-gather.6.cloned.1.call-start = ((), (), s32[]{:S(2)}) async-start(), calls=%async_computation.4 | async-start | bytes 10027008 | tf_op jit(solution)/shard_map/all_gather | solution.py:43
  13.3 27.0 %copy-start.28 = (bf16[2,512,512]{2,1,0:T(8,128)(2,1)}, bf16[2,512,512]{2,1,0:T(8,128)(2,1)S(1)}, u32[]{:S(2)}) copy-start(bf16[2,512,512]{2,1,0:T(8,128)(2,1)S(1)} %get-tuple-element.141) | copy-start | bytes 3145732
  13.3 27.0 %collective-permute-start.1 = (bf16[1024,512]{1,0:T(8,128)(2,1)S(1)}, bf16[1024,512]{1,0:T(8,128)(2,1)}, u32[]{:S(2)}, u32[]{:S(2)}) collective-permute-start(bf16[1024,512]{1,0:T(8,128)(2,1)S(1)} %bitcast.309), channel_id=1, source_target_pairs={{1,0},{0,1},{3,2},{2,3},{5,4},{4,5},{7,6},{6,7},{9,8},{8,9},{11,10... | collective-permute-start | bytes 3145736 | tf_op jit(solution)/shard_map/ppermute | solution.py:56
  16.2 45.7 %collective-permute-start = (bf16[1024,512]{1,0:T(8,128)(2,1)}, bf16[1024,512]{1,0:T(8,128)(2,1)}, u32[]{:S(2)}, u32[]{:S(2)}) collective-permute-start(bf16[1024,512]{1,0:T(8,128)(2,1)} %bitcast.1), channel_id=1, source_target_pairs={{1,0},{0,1},{3,2},{2,3},{5,4},{4,5},{7,6},{6,7},{9,8},{8,9},{11,10... | collective-permute-start | bytes 3145736 | tf_op jit(solution)/shard_map/ppermute | solution.py:56
  17.1 424.8 %reduce-scatter.6.cloned.1.call-start = ((), (), s32[]{:S(2)}) async-start(), calls=%async_computation.6 | async-start | bytes 5013504 | tf_op jit(solution)/shard_map/reduce_scatter | solution.py:47
  28.5 66.5 %copy-start.54 = (f32[1024,32]{0,1:T(8,128)}, f32[1024,32]{0,1:T(8,128)S(1)}, u32[]{:S(2)}) copy-start(f32[1024,32]{0,1:T(8,128)S(1)} %get-tuple-element.164) | copy-start | bytes 393220
  28.5 72.3 %copy-start.52 = (f32[1024,32]{0,1:T(8,128)}, f32[1024,32]{0,1:T(8,128)S(1)}, u32[]{:S(2)}) copy-start(f32[1024,32]{0,1:T(8,128)S(1)} %get-tuple-element.175) | copy-start | bytes 393220
  74.9 13.5 %copy-start.14 = (f32[1024,512]{0,1:T(8,128)}, f32[1024,512]{0,1:T(8,128)S(1)}, u32[]{:S(2)}) copy-start(f32[1024,512]{0,1:T(8,128)S(1)} %slice.203) | copy-start | bytes 6291460
  75.4 50.5 %copy-start.38 = (bf16[2,512,4,64]{1,0,3,2:T(2,128)(2,1)}, bf16[2,512,4,64]{1,0,3,2:T(2,128)(2,1)S(1)}, u32[]{:S(2)}) copy-start(bf16[2,512,4,64]{1,0,3,2:T(2,128)(2,1)S(1)} %reshape.461) | copy-start | bytes 1572868
  86.4 99.9 %copy-start.37 = (bf16[2,512,4,64]{1,0,3,2:T(2,128)(2,1)}, bf16[2,512,4,64]{1,0,3,2:T(2,128)(2,1)S(1)}, u32[]{:S(2)}) copy-start(bf16[2,512,4,64]{1,0,3,2:T(2,128)(2,1)S(1)} %reshape.464) | copy-start | bytes 1572868
  130.5 25.3 %copy-start.47 = (bf16[64,8,2,512]{3,1,2,0:T(8,128)(2,1)}, bf16[64,8,2,512]{3,1,2,0:T(8,128)(2,1)S(1)}, u32[]{:S(2)}) copy-start(bf16[64,8,2,512]{3,1,2,0:T(8,128)(2,1)S(1)} %copy.199) | copy-start | bytes 3145732
  131.5 24.3 %collective-permute-start.2 = (bf16[1024,512]{1,0:T(8,128)(2,1)S(1)}, bf16[1024,512]{1,0:T(8,128)(2,1)S(1)}, u32[]{:S(2)}, u32[]{:S(2)}) collective-permute-start(bf16[1024,512]{1,0:T(8,128)(2,1)S(1)} %convolution_convert_fusion.6), channel_id=1, source_target_pairs={{1,0},{0,1},{3,2},{2,3},{5,4},{4,5},{7,6},{6,7},{9,8},{8,9},{11,10... | collective-permute-start | bytes 3145736 | tf_op jit(solution)/shard_map/ppermute | solution.py:56
  133.4 22.4 %copy-start.25 = (bf16[2,512,1024]{2,1,0:T(8,128)(2,1)S(1)}, bf16[2,512,1024]{2,1,0:T(8,128)(2,1)}, u32[]{:S(2)}) copy-start(bf16[2,512,1024]{2,1,0:T(8,128)(2,1)} %get-tuple-element.115) | copy-start | bytes 6291460
  158.2 56.7 %collective-permute-start.3 = (bf16[1024,512]{1,0:T(8,128)(2,1)S(1)}, bf16[1024,512]{1,0:T(8,128)(2,1)S(1)}, u32[]{:S(2)}, u32[]{:S(2)}) collective-permute-start(bf16[1024,512]{1,0:T(8,128)(2,1)S(1)} %get-tuple-element.136), channel_id=1, source_target_pairs={{1,0},{0,1},{3,2},{2,3},{5,4},{4,5},{7,6},{6,7},{9,8},{8,9},{11,10... | collective-permute-start | bytes 3145736 | tf_op jit(solution)/shard_map/ppermute | solution.py:56
  189.6 25.3 %copy-start.32 = (bf16[2,512,4,2,64]{1,4,3,2,0:T(8,128)(2,1)}, bf16[2,512,4,2,64]{1,4,3,2,0:T(8,128)(2,1)S(1)}, u32[]{:S(2)}) copy-start(bf16[2,512,4,2,64]{1,4,3,2,0:T(8,128)(2,1)S(1)} %fusion.134) | copy-start | bytes 3145732
  190.9 26.0 %copy-start.49 = (bf16[64,8,2,512]{3,1,2,0:T(8,128)(2,1)}, bf16[64,8,2,512]{3,1,2,0:T(8,128)(2,1)S(1)}, u32[]{:S(2)}) copy-start(bf16[64,8,2,512]{3,1,2,0:T(8,128)(2,1)S(1)} %copy.201) | copy-start | bytes 3145732
  191.7 25.2 %collective-permute-start.5 = (bf16[1024,512]{1,0:T(8,128)(2,1)S(1)}, bf16[1024,512]{1,0:T(8,128)(2,1)S(1)}, u32[]{:S(2)}, u32[]{:S(2)}) collective-permute-start(bf16[1024,512]{1,0:T(8,128)(2,1)S(1)} %convolution_convert_fusion.5), channel_id=1, source_target_pairs={{1,0},{0,1},{3,2},{2,3},{5,4},{4,5},{7,6},{6,7},{9,8},{8,9},{11,10... | collective-permute-start | bytes 3145736 | tf_op jit(solution)/shard_map/ppermute | solution.py:56
  192.3 22.6 %collective-permute-start.4 = (f32[1024]{0:T(1024)S(1)}, f32[1024]{0:T(1024)S(1)}, u32[]{:S(2)}, u32[]{:S(2)}) collective-permute-start(f32[1024]{0:T(1024)S(1)} %get-tuple-element.135), channel_id=1, source_target_pairs={{1,0},{0,1},{3,2},{2,3},{5,4},{4,5},{7,6},{6,7},{9,8},{8,9},{11,10... | collective-permute-start | bytes 12296 | tf_op jit(solution)/shard_map/ppermute | solution.py:56
  193.8 98.4 %copy-start.111 = (f32[512]{0:T(512)}, f32[512]{0:T(512)S(1)}, u32[]{:S(2)}) copy-start(f32[512]{0:T(512)S(1)} %dynamic_slice.52) | copy-start | bytes 6148
  214.9 77.4 %copy-start.109 = (f32[1024]{0:T(1024)}, f32[1024]{0:T(1024)S(1)}, u32[]{:S(2)}) copy-start(f32[1024]{0:T(1024)S(1)} %add_rsqrt_fusion.5) | copy-start | bytes 12292
  217.7 48.7 %copy-start.3 = (f32[1024,512]{1,0:T(8,128)}, f32[1024,512]{1,0:T(8,128)S(1)}, u32[]{:S(2)}) copy-start(f32[1024,512]{1,0:T(8,128)S(1)} %convert_add_fusion) | copy-start | bytes 6291460
  256.7 12.1 %copy-start.124 = (bf16[1024,2304]{1,0:T(8,128)(2,1)S(1)}, bf16[1024,2304]{1,0:T(8,128)(2,1)}, u32[]{:S(2)}) copy-start(bf16[1024,2304]{1,0:T(8,128)(2,1)} %get-tuple-element.107) | copy-start | bytes 14155780
  265.9 26.3 %collective-permute-start.11 = (bf16[1024,512]{1,0:T(8,128)(2,1)S(1)}, bf16[1024,512]{1,0:T(8,128)(2,1)S(1)}, u32[]{:S(2)}, u32[]{:S(2)}) collective-permute-start(bf16[1024,512]{1,0:T(8,128)(2,1)S(1)} %fusion.121), channel_id=1, source_target_pairs={{1,0},{0,1},{3,2},{2,3},{5,4},{4,5},{7,6},{6,7},{9,8},{8,9},{11,10... | collective-permute-start | bytes 3145736 | tf_op jit(solution)/shard_map/ppermute | solution.py:56
  266.7 25.5 %collective-permute-start.7 = (f32[1024]{0:T(1024)S(1)}, f32[1024]{0:T(1024)S(1)}, u32[]{:S(2)}, u32[]{:S(2)}) collective-permute-start(f32[1024]{0:T(1024)S(1)} %get-tuple-element.131), channel_id=1, source_target_pairs={{1,0},{0,1},{3,2},{2,3},{5,4},{4,5},{7,6},{6,7},{9,8},{8,9},{11,10... | collective-permute-start | bytes 12296 | tf_op jit(solution)/shard_map/ppermute | solution.py:56
  268.4 46.3 %collective-permute-start.6 = (bf16[1024,512]{1,0:T(8,128)(2,1)S(1)}, bf16[1024,512]{1,0:T(8,128)(2,1)S(1)}, u32[]{:S(2)}, u32[]{:S(2)}) collective-permute-start(bf16[1024,512]{1,0:T(8,128)(2,1)S(1)} %get-tuple-element.132), channel_id=1, source_target_pairs={{1,0},{0,1},{3,2},{2,3},{5,4},{4,5},{7,6},{6,7},{9,8},{8,9},{11,10... | collective-permute-start | bytes 3145736 | tf_op jit(solution)/shard_map/ppermute | solution.py:56
  268.8 23.5 %copy-start.23 = (f32[1024,512]{1,0:T(8,128)S(1)}, f32[1024,512]{1,0:T(8,128)}, u32[]{:S(2)}) copy-start(f32[1024,512]{1,0:T(8,128)} %copy-done.22) | copy-start | bytes 6291460
  274.2 138.7 %collective-permute-start.9 = (bf16[1024,512]{1,0:T(8,128)(2,1)}, bf16[1024,512]{1,0:T(8,128)(2,1)S(1)}, u32[]{:S(2)}, u32[]{:S(2)}) collective-permute-start(bf16[1024,512]{1,0:T(8,128)(2,1)} %fusion.124), channel_id=1, source_target_pairs={{1,0},{0,1},{3,2},{2,3},{5,4},{4,5},{7,6},{6,7},{9,8},{8,9},{11,10... | collective-permute-start | bytes 3145736 | tf_op jit(solution)/shard_map/ppermute | solution.py:56
  292.2 23.2 %slice-start = ((s8[9437184]{0:T(1024)(128)(4,1)}), s8[4194304]{0:T(1024)(128)(4,1)S(1)}, s32[]{:S(2)}) async-start(s8[9437184]{0:T(1024)(128)(4,1)} %bitcast.368), calls=%async_computation.9 | async-start | bytes 8388608
  292.2 23.2 %slice-start.1 = ((s8[9437184]{0:T(1024)(128)(4,1)}), s8[4194304]{0:T(1024)(128)(4,1)S(1)}, s32[]{:S(2)}) async-start(s8[9437184]{0:T(1024)(128)(4,1)} %bitcast.368), calls=%async_computation.10 | async-start | bytes 8388608
  292.2 23.2 %slice-start.2 = ((s8[9437184]{0:T(1024)(128)(4,1)}), s8[1048576]{0:T(1024)(128)(4,1)S(1)}, s32[]{:S(2)}) async-start(s8[9437184]{0:T(1024)(128)(4,1)} %bitcast.368), calls=%async_computation.11 | async-start | bytes 2097152
  292.2 12.2 %copy-start.79 = (bf16[1024,512]{1,0:T(8,128)(2,1)}, bf16[1024,512]{1,0:T(8,128)(2,1)S(1)}, u32[]{:S(2)}) copy-start(bf16[1024,512]{1,0:T(8,128)(2,1)S(1)} %collective-permute-done.11) | copy-start | bytes 3145732
  304.5 115.2 %collective-permute-start.12 = (f32[1024]{0:T(1024)S(1)}, f32[1024]{0:T(1024)S(1)}, u32[]{:S(2)}, u32[]{:S(2)}) collective-permute-start(f32[1024]{0:T(1024)S(1)} %get-tuple-element.89), channel_id=1, source_target_pairs={{1,0},{0,1},{3,2},{2,3},{5,4},{4,5},{7,6},{6,7},{9,8},{8,9},{11,10... | collective-permute-start | bytes 12296 | tf_op jit(solution)/shard_map/ppermute | solution.py:56
  315.4 20.1 %slice-start.6 = ((s8[4718592]{0:T(1024)(128)(4,1)}), s8[524288]{0:T(1024)(128)(4,1)S(1)}, s32[]{:S(2)}) async-start(s8[4718592]{0:T(1024)(128)(4,1)} %bitcast.372), calls=%async_computation.15 | async-start | bytes 1048576
  322.8 12.7 %copy-start.73 = (bf16[1024,1024]{1,0:T(8,128)(2,1)S(1)}, bf16[1024,1024]{1,0:T(8,128)(2,1)}, u32[]{:S(2)}) copy-start(bf16[1024,1024]{1,0:T(8,128)(2,1)} %get-tuple-element.36) | copy-start | bytes 6291460
  322.8 12.7 %copy-start.75 = (bf16[1024,1024]{1,0:T(8,128)(2,1)S(1)}, bf16[1024,1024]{1,0:T(8,128)(2,1)}, u32[]{:S(2)}) copy-start(bf16[1024,1024]{1,0:T(8,128)(2,1)} %get-tuple-element.30) | copy-start | bytes 6291460
  322.8 12.7 %slice-start.7 = ((s8[4718592]{0:T(1024)(128)(4,1)}), s8[4194304]{0:T(1024)(128)(4,1)S(1)}, s32[]{:S(2)}) async-start(s8[4718592]{0:T(1024)(128)(4,1)} %bitcast.372), calls=%async_computation.16 | async-start | bytes 8388608
  348.8 230.8 %reduce-scatter.8.cloned.1.call-start = ((), (), s32[]{:S(2)}) async-start(), calls=%async_computation.7 | async-start | bytes 10027008 | tf_op jit(solution)/shard_map/reduce_scatter | solution.py:47
  355.7 64.0 %collective-permute-start.10 = (bf16[1024,512]{1,0:T(8,128)(2,1)}, bf16[1024,512]{1,0:T(8,128)(2,1)}, u32[]{:S(2)}, u32[]{:S(2)}) collective-permute-start(bf16[1024,512]{1,0:T(8,128)(2,1)} %fusion.127), channel_id=1, source_target_pairs={{1,0},{0,1},{3,2},{2,3},{5,4},{4,5},{7,6},{6,7},{9,8},{8,9},{11,10... | collective-permute-start | bytes 3145736 | tf_op jit(solution)/shard_map/ppermute | solution.py:56
  356.1 14.4 %copy-start.69 = (bf16[1024,1024]{1,0:T(8,128)(2,1)S(1)}, bf16[1024,1024]{1,0:T(8,128)(2,1)}, u32[]{:S(2)}) copy-start(bf16[1024,1024]{1,0:T(8,128)(2,1)} %multiply_convert_fusion.7) | copy-start | bytes 6291460
  411.2 16.9 %collective-permute-start.8 = (bf16[1024,512]{1,0:T(8,128)(2,1)S(1)}, bf16[1024,512]{1,0:T(8,128)(2,1)}, u32[]{:S(2)}, u32[]{:S(2)}) collective-permute-start(bf16[1024,512]{1,0:T(8,128)(2,1)S(1)} %fusion.118), channel_id=1, source_target_pairs={{1,0},{0,1},{3,2},{2,3},{5,4},{4,5},{7,6},{6,7},{9,8},{8,9},{11,10... | collective-permute-start | bytes 3145736 | tf_op jit(solution)/shard_map/ppermute | solution.py:56
  440.2 25.1 %collective-permute-start.13 = (bf16[1024,512]{1,0:T(8,128)(2,1)}, bf16[1024,512]{1,0:T(8,128)(2,1)}, u32[]{:S(2)}, u32[]{:S(2)}) collective-permute-start(bf16[1024,512]{1,0:T(8,128)(2,1)} %get-tuple-element.104), channel_id=1, source_target_pairs={{1,0},{0,1},{3,2},{2,3},{5,4},{4,5},{7,6},{6,7},{9,8},{8,9},{11,10... | collective-permute-start | bytes 3145736 | tf_op jit(solution)/shard_map/ppermute | solution.py:56
  443.8 18.2 %copy-start.29 = (bf16[2,512,512]{2,1,0:T(8,128)(2,1)S(1)}, bf16[2,512,512]{2,1,0:T(8,128)(2,1)}, u32[]{:S(2)}) copy-start(bf16[2,512,512]{2,1,0:T(8,128)(2,1)} %copy-done.28) | copy-start | bytes 3145732
  443.8 209.1 %reduce-scatter.10.cloned.1.call-start = ((), (), s32[]{:S(2)}) async-start(), calls=%async_computation.8 | async-start | bytes 3342336
  443.8 18.1 %collective-permute-start.16 = (f32[1024]{0:T(1024)S(1)}, f32[1024]{0:T(1024)S(1)}, u32[]{:S(2)}, u32[]{:S(2)}) collective-permute-start(f32[1024]{0:T(1024)S(1)} %get-tuple-element.172), channel_id=1, source_target_pairs={{1,0},{0,1},{3,2},{2,3},{5,4},{4,5},{7,6},{6,7},{9,8},{8,9},{11,10... | collective-permute-start | bytes 12296 | tf_op jit(solution)/shard_map/ppermute | solution.py:56
  444.5 17.4 %copy-start.20 = (f32[1024,512]{1,0:T(8,128)S(1)}, f32[1024,512]{1,0:T(8,128)}, u32[]{:S(2)}) copy-start(f32[1024,512]{1,0:T(8,128)} %copy-done.19) | copy-start | bytes 6291460
  463.5 44.0 %collective-permute-start.17 = (bf16[1024,512]{1,0:T(8,128)(2,1)}, bf16[1024,512]{1,0:T(8,128)(2,1)}, u32[]{:S(2)}, u32[]{:S(2)}) collective-permute-start(bf16[1024,512]{1,0:T(8,128)(2,1)} %fusion.219), channel_id=1, source_target_pairs={{1,0},{0,1},{3,2},{2,3},{5,4},{4,5},{7,6},{6,7},{9,8},{8,9},{11,10... | collective-permute-start | bytes 3145736 | tf_op jit(solution)/shard_map/ppermute | solution.py:56
  569.7 22.1 %collective-permute-start.14 = (bf16[1024,512]{1,0:T(8,128)(2,1)}, bf16[1024,512]{1,0:T(8,128)(2,1)}, u32[]{:S(2)}, u32[]{:S(2)}) collective-permute-start(bf16[1024,512]{1,0:T(8,128)(2,1)} %convolution_convert_fusion.2), channel_id=1, source_target_pairs={{1,0},{0,1},{3,2},{2,3},{5,4},{4,5},{7,6},{6,7},{9,8},{8,9},{11,10... | collective-permute-start | bytes 3145736 | tf_op jit(solution)/shard_map/ppermute | solution.py:56
  589.8 17.7 %collective-permute-start.18 = (bf16[1024,512]{1,0:T(8,128)(2,1)}, bf16[1024,512]{1,0:T(8,128)(2,1)}, u32[]{:S(2)}, u32[]{:S(2)}) collective-permute-start(bf16[1024,512]{1,0:T(8,128)(2,1)} %convolution_convert_fusion), channel_id=1, source_target_pairs={{1,0},{0,1},{3,2},{2,3},{5,4},{4,5},{7,6},{6,7},{9,8},{8,9},{11,10... | collective-permute-start | bytes 3145736 | tf_op jit(solution)/shard_map/ppermute | solution.py:56
  591.8 15.7 %copy-start.67 = (bf16[1024,1024]{1,0:T(8,128)(2,1)S(1)}, bf16[1024,1024]{1,0:T(8,128)(2,1)}, u32[]{:S(2)}) copy-start(bf16[1024,1024]{1,0:T(8,128)(2,1)} %slice.155) | copy-start | bytes 6291460
  591.8 15.7 %copy-start.90 = (bf16[1024,4,128]{0,2,1:T(8,128)(2,1)S(1)}, bf16[1024,4,128]{0,2,1:T(8,128)(2,1)}, u32[]{:S(2)}) copy-start(bf16[1024,4,128]{0,2,1:T(8,128)(2,1)} %copy-done.89) | copy-start | bytes 3145732
  591.8 15.7 %copy-start.95 = (bf16[1024,512]{0,1:T(8,128)(2,1)S(1)}, bf16[1024,512]{0,1:T(8,128)(2,1)}, u32[]{:S(2)}) copy-start(bf16[1024,512]{0,1:T(8,128)(2,1)} %copy-done.94) | copy-start | bytes 3145732
  596.6 13.5 %copy-start.13 = (bf16[2,512,1024]{2,1,0:T(8,128)(2,1)S(1)}, bf16[2,512,1024]{2,1,0:T(8,128)(2,1)}, u32[]{:S(2)}) copy-start(bf16[2,512,1024]{2,1,0:T(8,128)(2,1)} %copy-done.11) | copy-start | bytes 6291460
  596.6 13.5 %copy-start.26 = (bf16[2,512,1024]{2,1,0:T(8,128)(2,1)S(1)}, bf16[2,512,1024]{2,1,0:T(8,128)(2,1)}, u32[]{:S(2)}) copy-start(bf16[2,512,1024]{2,1,0:T(8,128)(2,1)} %get-tuple-element.115) | copy-start | bytes 6291460
  596.6 13.5 %copy-start.34 = (f32[1024,512]{1,0:T(8,128)S(1)}, f32[1024,512]{1,0:T(8,128)}, u32[]{:S(2)}) copy-start(f32[1024,512]{1,0:T(8,128)} %get-tuple-element.105) | copy-start | bytes 6291460
  596.6 13.5 %copy-start.106 = (f32[1,4,2,128]{3,1,2,0:T(4,128)S(1)}, f32[1,4,2,128]{3,1,2,0:T(4,128)}, u32[]{:S(2)}) copy-start(f32[1,4,2,128]{3,1,2,0:T(4,128)} %copy-done.105) | copy-start | bytes 12292
  596.6 13.5 %collective-permute-start.15 = (f32[1024]{0:T(1024)S(1)}, f32[1024]{0:T(1024)S(1)}, u32[]{:S(2)}, u32[]{:S(2)}) collective-permute-start(f32[1024]{0:T(1024)S(1)} %get-tuple-element.95), channel_id=1, source_target_pairs={{1,0},{0,1},{3,2},{2,3},{5,4},{4,5},{7,6},{6,7},{9,8},{8,9},{11,10... | collective-permute-start | bytes 12296 | tf_op jit(solution)/shard_map/ppermute | solution.py:56
  611.9 3.7 collective-permute-start.20
  612.4 6.2 collective-permute-start.19
  615.7 1.5 collective-permute-start.21
  617.2 3.9 collective-permute-start.22
  621.1 3.7 collective-permute-start.23
  624.8 4.7 collective-permute-start.24
  (101 other events, 488.9 us)
Sparse Core Ops, SparseCore 0:
  10.9 48.1 all-gather.3
  61.3 52.1 all-gather.7
  116.4 79.9 all-gather.5
  349.0 75.2 reduce-scatter.5
  443.9 110.8 reduce-scatter.7
  585.8 67.0 reduce-scatter.9
